TPU v7x, 32 devices: a whole 2x2x4 slice. The times are simulated.
32 devices in a mesh: row: 8 (over z, core), col: 4 (over y, x).
Axes of the slice: x: 2, y: 2, z: 4, core: 2. Of those that a mesh axis runs over, the one named last changes fastest.
Arguments:
- features: bfloat16 [8192, 128], P(('col', 'row')), may hold values from -96 to 96
- weight: bfloat16 [128, 256], replicated, may hold values from -0.5 to 0.5
- bias: float32 [256], replicated, may hold values from -3 to 3
- cotangent: bfloat16 [8192, 256], P(('row', 'col')), may hold values from -6 to 6
- tile_values: bfloat16 [8, 4, 128, 128, 128], P('row', 'col'), may hold values from 0 to 4, as said below
- tile_pos: int32 [8, 4, 2, 128], P('row', 'col'), may hold values from 0 to 15, as said below
- tile_count: int32 [8, 4], P('row', 'col'), may hold values from 0 to 128, as said below
- block_perm: int32 [64], replicated, may hold values from 0 to 63, as said below
Outputs:
- hidden: bfloat16 [8192, 256], P(('row', 'col'))
- weight_grad: float32 [128, 256], replicated
- bias_grad: float32 [256], replicated
Inputs may be any that keep to these rules, and one draw needn't show every extreme that they name: `tile_values`: entries are 0 or a weight of at least 0.25; slots t at or beyond tile_count[r, c] belong to no tile. `tile_pos`: entry [r, c, 0, t] is the slot's tile row, below 8, within row block r, and [r, c, 1, t] its tile column, below 16, within column block c, both in the reordered numbering; the slots of one cell hold distinct positions. `tile_count`: every draw has a cell with 128 live slots. `block_perm`: each aligned run of 8 entries is a permutation of that run's own indices.
All inputs are finite; a program needn't handle non-finite values.
Results may differ from a plain program's by a relative error of at most 0.0059.
Values may be sent and summed in bfloat16 or wider, within the bound.
A program may use at most 64 MiB of HBM per device.

v0:
```python
import jax
import jax.numpy as jnp
from jax import lax
from jax.sharding import PartitionSpec as P


def local_index(block_perm, tile_axis, block_index, run_length):
    return jnp.take(block_perm, block_index * run_length + tile_axis) - block_index * run_length


def body(features, weight, bias, cotangent, tile_values, tile_pos, tile_count, block_perm):
    row_count = lax.axis_size("row")
    col_count = lax.axis_size("col")
    row_index = lax.axis_index("row")
    col_index = lax.axis_index("col")
    packed = tile_values[0, 0]
    positions = tile_pos[0, 0]
    live_count = tile_count[0, 0]
    max_tiles = packed.shape[0]
    tile_size = packed.shape[1]
    feat_width = features.shape[1]
    row_tiles = block_perm.shape[0] // row_count
    col_tiles = row_tiles * row_count // col_count
    block_tiles = min(64, max_tiles)
    lane_index = jnp.arange(block_tiles, dtype=jnp.int32)
    own_rows = local_index(block_perm, positions[0], row_index, row_tiles)
    own_cols = local_index(block_perm, positions[1], col_index, col_tiles)

    def degree_step(block_step, totals):
        row_acc, col_acc = totals
        slot_number = block_step * block_tiles + lane_index
        is_live = slot_number < live_count
        clamped = jnp.minimum(slot_number, max_tiles - 1)
        values = jnp.take(packed, clamped, axis=0).astype(jnp.float32)
        row_part = jnp.sum(values, axis=2)
        col_part = jnp.sum(values, axis=1)
        row_part = jnp.where(is_live[:, None], row_part, 0.0)
        col_part = jnp.where(is_live[:, None], col_part, 0.0)
        row_acc = row_acc.at[jnp.take(own_rows, clamped)].add(row_part)
        col_acc = col_acc.at[jnp.take(own_cols, clamped)].add(col_part)
        return (row_acc, col_acc)

    degree_blocks = (live_count + block_tiles - 1) // block_tiles
    row_acc, col_acc = lax.fori_loop(
        jnp.int32(0),
        degree_blocks,
        degree_step,
        (
            jnp.zeros((row_tiles, tile_size), jnp.float32),
            jnp.zeros((col_tiles, tile_size), jnp.float32),
        ),
    )
    col_part_flat = col_acc.reshape(col_tiles * tile_size)
    raw_rows = lax.all_gather(features, "row", axis=0, tiled=True)
    col_total = lax.psum(col_part_flat, "row")
    gathered = (lax.rsqrt(1.0 + col_total)[:, None] * raw_rows.astype(jnp.float32)).astype(
        jnp.bfloat16
    )
    feature_tiles = gathered.reshape(col_tiles, tile_size, feat_width)
    list_length = packed.shape[0]

    def product_step(block_step, partial_value):
        logical = block_step * block_tiles + lane_index
        is_live = logical < live_count
        is_upper = logical >= live_count
        source = jnp.where(is_upper, logical - live_count, logical)
        source = jnp.clip(source, 0, list_length - 1)
        slot_number = jnp.minimum(is_upper.astype(jnp.int32), 1 - 1)
        tile_block = jnp.take(packed, source, axis=0)
        tile_block = jnp.where(is_live[:, None, None], tile_block, jnp.zeros((), jnp.bfloat16))
        inputs = jnp.take(feature_tiles, jnp.take(own_cols, source), axis=0)
        products = jnp.einsum(
            "bpq,bqf->bpf", tile_block, inputs, preferred_element_type=jnp.float32
        )
        return partial_value.at[slot_number, jnp.take(own_rows, source)].add(products)

    product_blocks = (live_count + block_tiles - 1) // block_tiles
    initial = jnp.zeros((1, row_tiles, tile_size, feat_width), jnp.float32)
    partial_value = lax.fori_loop(jnp.int32(0), product_blocks, product_step, initial)
    own_sum = partial_value[0]
    row_part_flat = row_acc.reshape(row_tiles * tile_size)
    summed, degree_share = (
        lax.psum_scatter(
            own_sum.reshape(row_tiles * tile_size, feat_width),
            "col",
            scatter_dimension=0,
            tiled=True,
        ),
        lax.psum_scatter(row_part_flat, "col", scatter_dimension=0, tiled=True),
    )
    aggregated = (lax.rsqrt(1.0 + degree_share)[:, None] * summed).astype(jnp.bfloat16)
    preact = jnp.dot(aggregated, weight, preferred_element_type=jnp.float32) + bias
    logistic = jax.nn.sigmoid(preact)
    hidden = (preact * logistic).astype(jnp.bfloat16)
    preact_grad = (
        cotangent.astype(jnp.float32) * logistic * (1.0 + preact * (1.0 - logistic))
    ).astype(jnp.bfloat16)
    weight_part = jnp.einsum(
        "nf,nh->fh", aggregated, preact_grad, preferred_element_type=jnp.float32
    )
    bias_part = jnp.sum(preact_grad.astype(jnp.float32), axis=0)
    weight_sum, bias_sum = lax.psum((weight_part, bias_part), ("row", "col"))
    inverse_root = lax.rsqrt(jnp.float32(summed.shape[0] * row_count * col_count))
    return (hidden, weight_sum * inverse_root, bias_sum * inverse_root)


def solution(mesh):
    placed = (
        P(("col", "row"), None),
        P(),
        P(),
        P(("row", "col"), None),
        P("row", "col", None, None, None),
        P("row", "col", None, None),
        P("row", "col"),
        P(),
    )
    return jax.shard_map(
        body,
        mesh=mesh,
        in_specs=placed,
        out_specs=(P(("row", "col"), None), P(), P()),
        check_vma=False,
    )
```

profile of v0, /device:TPU:0, one launch (start us, length us, event | category | flops | bytes accessed | tf_op | source)
XLA Modules:
  0.0 301.4 jit_solution(14471078804048986745)
XLA Ops:
  7.2 0.0 copy-start
  7.2 0.0 reduce-scatter.2.cloned.1.call-start
  7.9 0.8 compare_select_fusion.9
  8.7 1.6 gather_fusion.8
  10.2 1.6 gather_fusion.7
  11.8 0.8 fusion.31
  12.6 0.0 copy-start.2
  12.6 8.2 %while.24 = (s32[]{:T(128)}, f32[8,128]{1,0:T(8,128)S(1)}, f32[16,128]{1,0:T(8,128)S(1)}, s32[]{:T(128)}, s32[128]{0:T(128)S(1)}, /*index=5*/s32[]{:T(128)}, bf1...) while((s32[]{:T(128)}, f32[8,128]{1,0:T(8,128)S(1)}, ...), condition=%wide.region_5.9_spmd.clone, body=%wide.region_0.8_spmd.clone.sunk | while | flops 4213635 | bytes 6443601 | solution.py:44
  12.7 0.7 compare_and_fusion.6
  13.4 0.8 gather_fusion.1
  14.1 0.8 gather_fusion
  14.9 3.1 %gather_fusion.2 = bf16[64,128,128]{2,1,0:T(8,128)(2,1)S(1)} fusion(bf16[128,128,128]{2,1,0:T(8,128)(2,1)} %get-tuple-element.346, s32[1024]{0:T(1024)S(1)} %pad_clamp_fusion.8), kind=kCustom, calls=%fused_computation.2.clone.clone.1 | custom fusion | bytes 4194560 | tf_op jit(solution)/shard_map/while/body/jit(_take)/gather | solution.py:34
  18.1 0.9 convert_reduce_fusion.4
  18.9 1.0 scatter_custom_fusion.15
  19.9 1.0 scatter_custom_fusion.16
  20.9 22.5 %psum.21 = f32[2048]{0:T(1024)S(1)} all-reduce(f32[2048]{0:T(1024)S(1)} %bitcast.49), channel_id=1, replica_groups=mesh['row'=8,'col'=4] {'row'}, use_global_device_ids=true, to_apply=%region_7.11 | all-reduce | flops 2048 | bytes 16384 | tf_op jit(solution)/shard_map/psum | solution.py:55
  43.4 0.0 copy-done.2
  43.4 15.0 %all_gather.3 = bf16[2048,128]{1,0:T(8,128)(2,1)S(1)} all-gather(bf16[256,128]{1,0:T(8,128)(2,1)S(1)} %copy-done.2), channel_id=1, replica_groups=mesh['row'=8,'col'=4] {'row'}, dimensions={0}, use_global_device_ids=true | all-gather | bytes 589824 | tf_op jit(solution)/shard_map/all_gather | solution.py:54
  58.4 0.3 multiply_convert_fusion
  58.8 0.0 copy-start.5
  58.8 0.0 copy-start.3
  58.8 0.0 copy-start.4
  58.9 21.4 %while.25 = (s32[]{:T(128)}, f32[1,8,128,128]{3,2,1,0:T(8,128)S(1)}, s32[]{:T(128)}, s32[]{:T(128)}, s32[128]{0:T(128)S(1)}, /*index=5*/bf16[128,128,128]{2,1,0:...) while((s32[]{:T(128)}, ...), condition=%wide.region_10.14_spmd.clone, body=%wide.region_8.13_spmd.clone.sunk | while | flops 272634240 | bytes 29373440 | solution.py:79
  58.9 0.7 compare_and_fusion.7
  59.6 0.8 gather_fusion.5
  60.4 0.8 gather_fusion.3
  61.2 0.7 fusion.43
  61.8 1.0 gather_fusion.6
  62.8 4.3 %gather_fusion.4 = bf16[64,128,128]{2,1,0:T(8,128)(2,1)} fusion(bf16[128,128,128]{2,1,0:T(8,128)(2,1)} %get-tuple-element.376, s32[1024]{0:T(1024)S(1)} %pad_clamp_fusion.9), kind=kCustom, calls=%fused_computation.7.clone.clone.1 | custom fusion | bytes 4194560 | tf_op jit(solution)/shard_map/while/body/jit(_take)/gather | solution.py:69
  67.1 4.3 %fusion.44 = f32[64,128,128]{2,1,0:T(8,128)} fusion(bf16[64,128,128]{2,1,0:T(8,128)(2,1)} %gather_fusion.4, bf16[64,128,128]{2,1,0:T(8,128)(2,1)S(1)} %gather_fusion.6, pred[64]{0:T(512)(128)(4,1)S(1)} %get-tuple-element.315, pred[64]{0:T(512)(128)(4,1)S(1)} %get-tuple-element.316, pred[64]{0:T(512)(128)(4,1)S(1)} %get-tuple-element.317), kind=kOutput, calls=%fused_computation.34.clone.1 | convolution fusion | flops 271581184 | bytes 8388800 | tf_op jit(solution)/shard_map/while/body/bpq,bqf->bpf/dot_general | solution.py:72
  71.4 8.8 %scatter_fusion = f32[8,128,128]{2,1,0:T(8,128)S(1)} fusion(f32[8,128,128]{2,1,0:T(8,128)S(1)} %bitcast.44, s32[64]{0:T(128)S(1)} %fusion.43, f32[64,128,128]{2,1,0:T(8,128)} %fusion.44), kind=kCustom, calls=%fused_computation.11.clone.clone.1 | custom fusion | flops 1048576 | bytes 12583168 | tf_op jit(solution)/shard_map/while/body/scatter-add | solution.py:75
  80.2 0.0 copy-start.1
  80.3 0.8 copy-done.1
  81.0 0.0 reduce-scatter.2.cloned.1.call-update
  81.1 0.0 all-reduce.3.cloned.1.call-start
  81.1 0.0 copy-done.5
  81.1 0.6 dynamic-slice
  82.4 32.4 %all-reduce = f32[1024]{0:T(1024)S(1)} all-reduce(f32[1024]{0:T(1024)S(1)} %bitcast.50), channel_id=2, replica_groups=mesh['row'=8,'col'=4] {'col'}, use_global_device_ids=true, to_apply=%region_6.10.clone | all-reduce | flops 1024 | bytes 8192
  114.7 0.1 fusion.29
  114.8 11.8 %reduce-scatter.2.cloned.1.call-done = f32[256,128]{1,0:T(8,128)} async-done(((f32[1024,128]{1,0:T(8,128)}), f32[256,128]{1,0:T(8,128)}) %reduce-scatter.2.cloned.1.call-update) | async-done | bytes 131088 | tf_op jit(solution)/shard_map/reduce_scatter | solution.py:83
  126.6 0.0 copy-done
  126.6 0.0 copy-done.3
  126.6 0.0 copy-done.4
  126.6 1.9 convert_reduce_fusion.2
  128.5 39.3 %psum.23 = f32[256]{0:T(256)S(1)} all-reduce(f32[256]{0:T(256)S(1)} %get-tuple-element.182), channel_id=1, replica_groups=mesh['row'=8,'col'=4] {'row','col'}, use_global_device_ids=true, to_apply=%region_14.18 | all-reduce | flops 256 | bytes 2048 | tf_op jit(solution)/shard_map/psum | solution.py:102
  167.8 1.8 fusion.32
  169.6 0.0 all-reduce.3.cloned.1.call-update
  169.7 0.6 broadcast_multiply_fusion.1
  170.2 122.8 %all-reduce.3.cloned.1.call-done = f32[128,256]{1,0:T(8,128)} async-done(((f32[128,256]{1,0:T(8,128)}), f32[128,256]{1,0:T(8,128)}) %all-reduce.3.cloned.1.call-update) | async-done | bytes 131088 | tf_op jit(solution)/shard_map/psum | solution.py:102
  293.0 1.6 broadcast_multiply_fusion
  (11 shorter events, 0.1 us)
Async XLA Ops:
  7.2 119.5 %copy-start = (bf16[128,256]{1,0:T(8,128)(2,1)S(1)}, bf16[128,256]{1,0:T(8,128)(2,1)}, u32[]{:S(2)}) copy-start(bf16[128,256]{1,0:T(8,128)(2,1)} %param.19) | copy-start | bytes 196612
  7.2 119.5 %reduce-scatter.2.cloned.1.call-start = ((), (), s32[]{:S(2)}) async-start(), calls=%async_computation.1 | async-start | bytes 655360 | tf_op jit(solution)/shard_map/reduce_scatter | solution.py:83
  12.6 30.8 %copy-start.2 = (bf16[256,128]{1,0:T(8,128)(2,1)S(1)}, bf16[256,128]{1,0:T(8,128)(2,1)}, u32[]{:S(2)}) copy-start(bf16[256,128]{1,0:T(8,128)(2,1)} %param.18) | copy-start | bytes 196612
  58.8 22.3 %copy-start.5 = (u32[32]{0:T(128)S(1)}, u32[32]{0:T(128)}, u32[]{:S(2)}) copy-start(u32[32]{0:T(128)} %constant.128) | copy-start | bytes 388
  58.8 67.8 %copy-start.3 = (bf16[256,256]{1,0:T(8,128)(2,1)S(1)}, bf16[256,256]{1,0:T(8,128)(2,1)}, u32[]{:S(2)}) copy-start(bf16[256,256]{1,0:T(8,128)(2,1)} %param.21) | copy-start | bytes 393220
  58.8 67.8 %copy-start.4 = (f32[256]{0:T(256)S(1)}, f32[256]{0:T(256)}, u32[]{:S(2)}) copy-start(f32[256]{0:T(256)} %param.20) | copy-start | bytes 3076
  80.2 0.8 copy-start.1
  81.1 212.0 %all-reduce.3.cloned.1.call-start = ((), (), s32[]{:S(2)}) async-start(), calls=%async_computation.2 | async-start | bytes 262144 | tf_op jit(solution)/shard_map/psum | solution.py:102
Sparse Core Ops, SparseCore 0:
  81.2 45.4 reduce-scatter.1
  169.8 123.1 all-reduce.2
where the time goes:
time: 303 us; the launch traced here: 301 us
  waiting for transfers between devices  135 us (45%)
  blocking collectives  109 us (36%)
  other arithmetic  17.7 us (6%)
  local copies, waits for them, and re-layouts  16.2 us (5%)
  between operations  15.5 us (5%)
  matrix products  8.04 us (3%)
    psum x1, waiting for transfers between devices, body(): weight_sum, bias_sum = lax.psum((weight_part, bias_part), ('row', 'col'))  123 us
    psum x1, blocking collectives, body(): weight_sum, bias_sum = lax.psum((weight_part, bias_part), ('row', 'col'))  39.3 us
    unnamed x1, blocking collectives  32.4 us
    psum x1, blocking collectives, body(): col_total = lax.psum(col_part_flat, 'row')  22.5 us
    all_gather x1, blocking collectives, body(): raw_rows = lax.all_gather(features, 'row', axis=0, tiled=True)  15 us
    reduce_scatter x1, waiting for transfers between devices, body(): lax.psum_scatter(own_sum.reshape(row_tiles * tile_size, feat_width), 'col...  11.8 us
    scatter-add x1, other arithmetic, product_step(): partial_value.at[slot_number, jnp.take(own_rows, source)].add(products)  8.78 us
  transfers between devices with their start and end apart: 2, of which 2 were waited for; matrix products, arithmetic and copies ran while one was open for 0% of the time, Pallas kernels for 0%

commit v1 on v0

v1 whole, which is shorter than its diff:
```python
import functools

import jax
import jax.numpy as jnp
from jax import lax
from jax.experimental import pallas as pl
from jax.experimental.pallas import tpu as pltpu
from jax.sharding import PartitionSpec as P

MESH = pl.DeviceIdType.MESH
F32 = jnp.float32
BF16 = jnp.bfloat16
WIRE = jnp.float32
TILE_ROWS = 8
LANES = 128


def kernel(
    row_count,
    col_count,
    feat_ref,
    weight_ref,
    bias_ref,
    cot_ref,
    tiles_hbm,
    pos_ref,
    count_ref,
    perm_ref,
    hidden_ref,
    wgrad_ref,
    bgrad_ref,
    tiles,
    dense,
    index_vmem,
    index_smem,
    gathered,
    scaled,
    col_buf,
    row_send,
    row_buf,
    prod_send,
    prod_buf,
    grad_send,
    grad_buf,
    out_buf,
    tile_sem,
    index_sem,
    feat_send_sem,
    feat_recv_sem,
    small_send_sem,
    small_recv_sem,
):
    row = lax.axis_index("row")
    col = lax.axis_index("col")
    device_count = row_count * col_count
    me = row * col_count + col
    core = lax.rem(row, 2)
    chip = row // 2
    chips = row_count // 2
    sibling = row + 1 - 2 * core
    max_tiles = tiles.shape[0] - 1
    tile = tiles.shape[1]
    row_tiles = dense.shape[0] // tile
    col_tiles = dense.shape[1] // tile
    own_rows = hidden_ref.shape[0]
    feat_rows, feat_width = feat_ref.shape
    hidden_width = weight_ref.shape[1]
    grad_tiles = out_buf.shape[0]
    halves = hidden_width // LANES

    tile_copy = pltpu.make_async_copy(
        tiles_hbm.at[0, 0], tiles.at[pl.ds(0, max_tiles)], tile_sem
    )
    tile_copy.start()

    barrier = pltpu.get_barrier_semaphore()

    def greet(step, carry):
        other = lax.rem(me + step, device_count)
        pl.semaphore_signal(
            barrier,
            inc=1,
            device_id=(other // col_count, lax.rem(other, col_count)),
            device_id_type=MESH,
        )
        return carry

    lax.fori_loop(1, device_count, greet, 0)

    tile_row = pos_ref[0, 0, 0:1, :]
    tile_col = pos_ref[0, 0, 1:2, :]
    code_row = jnp.zeros((1, max_tiles), jnp.int32)
    for i in range(row_tiles):
        place = perm_ref[row * row_tiles + i] - row * row_tiles
        code_row = jnp.where(tile_row == i, place, code_row)
    code_col = jnp.zeros((1, max_tiles), jnp.int32)
    for j in range(col_tiles):
        place = perm_ref[col * col_tiles + j] - col * col_tiles
        code_col = jnp.where(tile_col == j, place, code_col)
    slot_lane = lax.broadcasted_iota(jnp.int32, (1, max_tiles), 1)
    code = jnp.where(slot_lane < count_ref[0, 0], code_row * col_tiles + code_col, -1)
    code = jnp.transpose(jnp.broadcast_to(code, (LANES, max_tiles)))
    positions = row_tiles * col_tiles
    slot_sub = lax.broadcasted_iota(jnp.int32, (max_tiles, LANES), 0)
    for start in range(0, positions, LANES):
        place = lax.broadcasted_iota(jnp.int32, (max_tiles, LANES), 1) + start
        slot = jnp.min(jnp.where(code == place, slot_sub, max_tiles), axis=0, keepdims=True)
        index_vmem[:, start : start + LANES] = jnp.broadcast_to(slot, (8, LANES))
    index_copy = pltpu.make_async_copy(index_vmem, index_smem, index_sem)
    index_copy.start()
    tiles[max_tiles] = jnp.zeros((tile, tile), BF16)

    pl.semaphore_wait(barrier, device_count - 1)

    def feat_copy(source, source_row, target_row, send_slot):
        return pltpu.make_async_remote_copy(
            src_ref=source,
            dst_ref=gathered.at[source_row],
            send_sem=feat_send_sem.at[send_slot],
            recv_sem=feat_recv_sem.at[source_row],
            device_id=(target_row, col),
            device_id_type=MESH,
        )

    for step in range(1, chips):
        target = lax.rem(chip + step, chips) * 2 + core
        feat_copy(feat_ref, row, target, step).start()
    feat_copy(feat_ref, row, sibling, 0).start()
    gathered[row] = feat_ref[...]

    tile_copy.wait()
    index_copy.wait()

    def build(b, carry):
        columns = pl.ds(pl.multiple_of(b * tile, tile), tile)
        total = jnp.zeros((tile, tile), F32)
        for a in range(row_tiles):
            block = tiles[index_smem[0, a * col_tiles + b]]
            dense[a * tile : (a + 1) * tile, columns] = block
            total = total + block.astype(F32)
        col_buf[row, pl.ds(b, 1), :] = jnp.sum(total, axis=0, keepdims=True)
        return carry

    lax.fori_loop(0, col_tiles, build, 0)

    def small_copy(source, target_ref, target_row, target_col, which):
        return pltpu.make_async_remote_copy(
            src_ref=source,
            dst_ref=target_ref,
            send_sem=small_send_sem.at[which],
            recv_sem=small_recv_sem.at[which],
            device_id=(target_row, target_col),
            device_id_type=MESH,
        )

    def wait_all(source, target_ref, which):
        copy = small_copy(source, target_ref, sibling, col, which)
        copy.wait_send()
        copy.wait_recv()

    for step in range(1, row_count):
        target = lax.rem(row + step, row_count)
        small_copy(col_buf.at[row], col_buf.at[row], target, col, 0).start()

    ones = jnp.ones((dense.shape[1], LANES), BF16)
    for k in range(col_count):
        for piece in range(own_rows // tile):
            at = k * own_rows + piece * tile
            sums = jnp.dot(dense[at : at + tile, :], ones, preferred_element_type=F32)
            row_send[k, :, piece * tile : (piece + 1) * tile] = jnp.transpose(sums)[0:8, :]
    for step in range(1, col_count):
        target = lax.rem(col + step, col_count)
        small_copy(row_send.at[target], row_buf.at[col], row, target, 1).start()
    row_buf[col] = row_send[col]

    for step in range(1, chips):
        source = lax.rem(chip + chips - step, chips) * 2 + core
        feat_copy(feat_ref, source, sibling, 0).wait_recv()
        feat_copy(gathered.at[source], source, sibling, chips + step - 1).start()

    wait_all(col_buf.at[pl.ds(0, row_count - 1)], col_buf.at[pl.ds(0, row_count - 1)], 0)
    col_total = col_buf[0]
    for r in range(1, row_count):
        col_total = col_total + col_buf[r]
    col_scale = lax.rsqrt(1.0 + col_total)
    col_scale = jnp.concatenate(
        [col_scale, jnp.zeros((LANES - col_tiles, tile), F32)], axis=0
    )
    col_scale = jnp.transpose(col_scale)

    wait_all(row_buf.at[pl.ds(0, col_count - 1)], row_buf.at[pl.ds(0, col_count - 1)], 1)
    row_total = row_buf[0]
    for c in range(1, col_count):
        row_total = row_total + row_buf[c]
    row_scale = lax.rsqrt(1.0 + row_total)
    row_scale = jnp.concatenate(
        [
            jnp.transpose(
                jnp.broadcast_to(row_scale[0:1, at : at + tile], (LANES, tile))
            )
            for at in range(0, own_rows, tile)
        ],
        axis=0,
    )

    feat_copy(feat_ref, sibling, sibling, 0).wait_recv()
    for step in range(1, chips):
        source = lax.rem(chip + chips - step, chips) * 2 + 1 - core
        feat_copy(feat_ref, source, sibling, 0).wait_recv()
    per_device = feat_rows // tile
    for j in range(col_tiles):
        at = (j % per_device) * tile
        block = gathered[j // per_device, at : at + tile, :].astype(F32)
        scaled[j * tile : (j + 1) * tile, :] = (col_scale[:, j : j + 1] * block).astype(BF16)

    def product(piece):
        rows = pl.ds(pl.multiple_of(piece * own_rows, own_rows), own_rows)
        return jnp.dot(dense[rows, :], scaled[...], preferred_element_type=F32)

    for step in range(1, col_count):
        target = lax.rem(col + step, col_count)
        prod_send[step - 1] = product(target).astype(WIRE)
        small_copy(prod_send.at[step - 1], prod_buf.at[col], row, target, 2).start()
    summed = product(col)
    prod_buf[col] = jnp.zeros((own_rows, feat_width), WIRE)
    wait_all(prod_send, prod_buf.at[pl.ds(0, col_count - 1)], 2)
    for c in range(col_count):
        summed = summed + prod_buf[c].astype(F32)

    aggregated = (row_scale * summed).astype(BF16)
    preact = jnp.dot(aggregated, weight_ref[...], preferred_element_type=F32) + bias_ref[...]
    logistic = jax.nn.sigmoid(preact)
    hidden_ref[...] = (preact * logistic).astype(BF16)
    preact_grad = (
        cot_ref[...].astype(F32) * logistic * (1.0 + preact * (1.0 - logistic))
    ).astype(BF16)
    weight_part = lax.dot_general(
        aggregated, preact_grad, (((0,), (0,)), ((), ())), preferred_element_type=F32
    )
    bias_part = jnp.sum(preact_grad.astype(F32), axis=0, keepdims=True)

    bias_rows = jnp.concatenate(
        [bias_part[:, h * LANES : (h + 1) * LANES] for h in range(halves)]
        + [jnp.zeros((TILE_ROWS - halves, LANES), F32)],
        axis=0,
    )
    for t in range(grad_tiles):
        i, h = t // halves, t % halves
        part = weight_part[i * TILE_ROWS : (i + 1) * TILE_ROWS, h * LANES : (h + 1) * LANES]
        grad_send[t] = jnp.concatenate([part, bias_rows], axis=0).astype(BF16)

    def send_part(step, carry):
        other = lax.rem(me + step, device_count)
        small_copy(
            grad_send.at[lax.rem(other, grad_tiles)],
            grad_buf.at[me],
            other // col_count,
            lax.rem(other, col_count),
            3,
        ).start()
        return carry

    lax.fori_loop(1, device_count, send_part, 0)
    own_tile = lax.rem(me, grad_tiles)
    grad_buf[me] = grad_send[own_tile]
    wait_all(
        grad_buf.at[pl.ds(0, device_count - 1)], grad_buf.at[pl.ds(0, device_count - 1)], 3
    )

    def add_part(d, total):
        return total + grad_buf[d].astype(F32)

    total = lax.fori_loop(0, device_count, add_part, jnp.zeros((2 * TILE_ROWS, LANES), F32))
    inverse_root = lax.rsqrt(F32(own_rows * device_count))
    total = total * inverse_root
    out_buf[own_tile] = total[0:TILE_ROWS]
    first = me - own_tile

    def send_total(step, carry):
        other = first + lax.rem(own_tile + step, grad_tiles)
        small_copy(
            out_buf.at[own_tile],
            out_buf.at[own_tile],
            other // col_count,
            lax.rem(other, col_count),
            4,
        ).start()
        return carry

    lax.fori_loop(1, grad_tiles, send_total, 0)
    for h in range(halves):
        bgrad_ref[:, h * LANES : (h + 1) * LANES] = total[TILE_ROWS + h : TILE_ROWS + h + 1]
    for step in range(1, chips):
        feat_copy(feat_ref, row, sibling, step).wait_send()
        feat_copy(feat_ref, row, sibling, chips + step - 1).wait_send()
    feat_copy(feat_ref, row, sibling, 0).wait_send()
    wait_all(out_buf.at[pl.ds(0, grad_tiles - 1)], out_buf.at[pl.ds(0, grad_tiles - 1)], 4)
    for t in range(grad_tiles):
        i, h = t // halves, t % halves
        wgrad_ref[i * TILE_ROWS : (i + 1) * TILE_ROWS, h * LANES : (h + 1) * LANES] = out_buf[t]


def solution(mesh):
    row_count = mesh.shape["row"]
    col_count = mesh.shape["col"]
    device_count = row_count * col_count

    def body(features, weight, bias, cotangent, tile_values, tile_pos, tile_count, block_perm):
        max_tiles, tile = tile_values.shape[2], tile_values.shape[3]
        row_tiles = block_perm.shape[0] // row_count
        col_tiles = block_perm.shape[0] // col_count
        feat_rows, feat_width = features.shape
        own_rows, hidden_width = cotangent.shape
        grad_tiles = feat_width * hidden_width // (TILE_ROWS * LANES)
        vmem = pl.BlockSpec(memory_space=pltpu.VMEM)
        smem = pl.BlockSpec(memory_space=pltpu.SMEM)
        hidden, weight_grad, bias_grad = pl.pallas_call(
            functools.partial(kernel, row_count, col_count),
            out_shape=(
                jax.ShapeDtypeStruct((own_rows, hidden_width), BF16),
                jax.ShapeDtypeStruct((feat_width, hidden_width), F32),
                jax.ShapeDtypeStruct((1, hidden_width), F32),
            ),
            in_specs=[vmem, vmem, vmem, vmem, pl.BlockSpec(memory_space=pl.ANY), vmem, smem, smem],
            out_specs=(vmem, vmem, vmem),
            scratch_shapes=[
                pltpu.VMEM((max_tiles + 1, tile, tile), BF16),
                pltpu.VMEM((row_tiles * tile, col_tiles * tile), BF16),
                pltpu.VMEM((8, row_tiles * col_tiles), jnp.int32),
                pltpu.SMEM((8, row_tiles * col_tiles), jnp.int32),
                pltpu.VMEM((row_count, feat_rows, feat_width), BF16),
                pltpu.VMEM((col_tiles * tile, feat_width), BF16),
                pltpu.VMEM((row_count, col_tiles, tile), F32),
                pltpu.VMEM((col_count, 8, own_rows), F32),
                pltpu.VMEM((col_count, 8, own_rows), F32),
                pltpu.VMEM((col_count - 1, own_rows, feat_width), WIRE),
                pltpu.VMEM((col_count, own_rows, feat_width), WIRE),
                pltpu.VMEM((grad_tiles, 2 * TILE_ROWS, LANES), BF16),
                pltpu.VMEM((device_count, 2 * TILE_ROWS, LANES), BF16),
                pltpu.VMEM((grad_tiles, TILE_ROWS, LANES), F32),
                pltpu.SemaphoreType.DMA,
                pltpu.SemaphoreType.DMA,
                pltpu.SemaphoreType.DMA((row_count,)),
                pltpu.SemaphoreType.DMA((row_count,)),
                pltpu.SemaphoreType.DMA((5,)),
                pltpu.SemaphoreType.DMA((5,)),
            ],
            compiler_params=pltpu.CompilerParams(
                collective_id=0, has_side_effects=True, vmem_limit_bytes=40 * 1024 * 1024
            ),
        )(
            features,
            weight,
            bias.reshape(1, hidden_width),
            cotangent,
            tile_values,
            tile_pos,
            tile_count,
            block_perm,
        )
        return hidden, weight_grad, bias_grad.reshape(hidden_width)

    return jax.shard_map(
        body,
        mesh=mesh,
        in_specs=(
            P(("col", "row"), None),
            P(),
            P(),
            P(("row", "col"), None),
            P("row", "col", None, None, None),
            P("row", "col", None, None),
            P("row", "col"),
            P(),
        ),
        out_specs=(P(("row", "col"), None), P(), P()),
        check_vma=False,
    )
```

time: 303 us -> 47.3 us (0.16)
  waiting for transfers between devices: 135 us -> 0 us
  blocking collectives: 109 us -> 0 us
  Pallas kernels: 0 us -> 36.9 us
  other arithmetic: 17.7 us -> 0 us
  between operations: 15.5 us -> 1.3 us
  matrix products: 8.04 us -> 0 us
  local copies, waits for them, and re-layouts: 16.2 us -> 8.65 us
    psum x1 -> x0, waiting for transfers between devices: 123 us -> none  [body(): weight_sum, bias_sum = lax.psum((weight_part, bias_part), ('row', 'col'))]
    psum x2 -> x0, blocking collectives: 61.8 us -> none  [the longest x1 39.3 us: body(): weight_sum, bias_sum = lax.psum((weight_part, bias_part), ('row', 'col'))]
    pallas_call x0 -> x1, Pallas kernels: none -> 36.9 us  [body(): pl.pallas_call(functools.partial(kernel, row_count, col_count), out_shape...]
    unnamed x1 -> x0, blocking collectives: 32.4 us -> none
    all_gather x1 -> x0, blocking collectives: 15 us -> none  [body(): raw_rows = lax.all_gather(features, 'row', axis=0, tiled=True)]
    gather x9 -> x0, local copies, waits for them, and re-layouts: 14.7 us -> none  [the longest x1 4.33 us: product_step(): tile_block = jnp.take(packed, source, axis=0)]
    reduce_scatter x1 -> x0, waiting for transfers between devices: 11.8 us -> none  [body(): lax.psum_scatter(own_sum.reshape(row_tiles * tile_size, feat_width), 'col...]
    scatter-add x3 -> x0, other arithmetic: 10.7 us -> none  [the longest x1 8.78 us: product_step(): partial_value.at[slot_number, jnp.take(own_rows, source)].add(products)]
  transfers between devices with their start and end apart: 2 -> 0, of which waited for: 2 -> 0; matrix products, arithmetic and copies ran while one was open for 0% -> 0% of each run, Pallas kernels for 0% -> 0%
where the time goes in v1:
time: 47.3 us; the launch traced here: 46.8 us
  Pallas kernels  36.9 us (78%)
  local copies, waits for them, and re-layouts  8.65 us (18%)
  between operations  1.3 us (3%)
    pallas_call x1, Pallas kernels, body(): pl.pallas_call(functools.partial(kernel, row_count, col_count), out_shape...  36.9 us
    unnamed x17, local copies, waits for them, and re-layouts  8.65 us

profile of v1, /device:TPU:0, one launch (start us, length us, event | category | flops | bytes accessed | tf_op | source)
XLA Modules:
  0.0 46.8 jit_solution(310599262351089114)
XLA Ops:
  1.3 0.0 copy-start
  1.3 2.2 %copy-done = bf16[1,1,128,128,128]{4,3,2,1,0:T(8,128)(2,1)S(1)} copy-done((bf16[1,1,128,128,128]{4,3,2,1,0:T(8,128)(2,1)S(1)}, bf16[1,1,128,128,128]{4,3,2,1,0:T(8,128)(2,1)}, u32[]{:S(2)}) %copy-start) | copy-done | bytes 4194328
  3.5 0.0 copy-start.1
  3.5 0.9 %copy-done.1 = bf16[256,256]{1,0:T(8,128)(2,1)S(1)} copy-done((bf16[256,256]{1,0:T(8,128)(2,1)S(1)}, bf16[256,256]{1,0:T(8,128)(2,1)}, u32[]{:S(2)}) %copy-start.1) | copy-done | bytes 131096
  4.4 0.0 copy-start.2
  4.4 0.8 %copy-done.2 = bf16[256,128]{1,0:T(8,128)(2,1)S(1)} copy-done((bf16[256,128]{1,0:T(8,128)(2,1)S(1)}, bf16[256,128]{1,0:T(8,128)(2,1)}, u32[]{:S(2)}) %copy-start.2) | copy-done | bytes 65560
  5.2 0.0 copy-start.3
  5.2 0.8 %copy-done.3 = bf16[128,256]{1,0:T(8,128)(2,1)S(1)} copy-done((bf16[128,256]{1,0:T(8,128)(2,1)S(1)}, bf16[128,256]{1,0:T(8,128)(2,1)}, u32[]{:S(2)}) %copy-start.3) | copy-done | bytes 65560
  6.1 0.0 copy-start.4
  6.1 0.7 %copy-done.4 = f32[256]{0:T(256)S(1)} copy-done((f32[256]{0:T(256)S(1)}, f32[256]{0:T(256)}, u32[]{:S(2)}) %copy-start.4) | copy-done | bytes 1048
  6.7 0.0 copy-start.5
  6.7 0.7 %copy-done.5 = s32[1,1,2,128]{3,2,1,0:T(2,128)S(1)} copy-done((s32[1,1,2,128]{3,2,1,0:T(2,128)S(1)}, s32[1,1,2,128]{3,2,1,0:T(2,128)}, u32[]{:S(2)}) %copy-start.5) | copy-done | bytes 1048
  7.4 0.0 copy-start.6
  7.4 0.7 %copy-done.6 = s32[64]{0:T(128)S(1)} copy-done((s32[64]{0:T(128)S(1)}, s32[64]{0:T(128)}, u32[]{:S(2)}) %copy-start.6) | copy-done | bytes 280
  8.1 36.9 %shard_map.103 = (bf16[256,256]{1,0:T(8,128)(2,1)S(1)}, f32[128,256]{1,0:T(8,128)S(1)}, f32[1,256]{1,0:T(1,128)S(1)}) custom-call(bf16[256,128]{1,0:T(8,128)(2,1)S(1)} %copy-done.2, bf16[128,256]{1,0:T(8,128)(2,1)S(1)} %copy-done.3, f32[1,256]{1,0:T(1,128)S(1)} %bitcast.2, bf16[256,256]{1,0:T(8,128)(2,1)S(1)} %copy-done.1, ...), custom_call_target="tpu_custom_call" | custom-call | tf_op jit(solution)/shard_map/pallas_call | solution.py:317
  44.9 0.7 %copy.15 = bf16[256,256]{1,0:T(8,128)(2,1)} copy(bf16[256,256]{1,0:T(8,128)(2,1)S(1)} %get-tuple-element.12) | data formatting | bytes 262144
  45.6 0.7 %copy.16 = f32[128,256]{1,0:T(8,128)} copy(f32[128,256]{1,0:T(8,128)S(1)} %get-tuple-element.13) | data formatting | bytes 262144
  46.2 0.6 %copy.17 = f32[256]{0:T(256)} copy(f32[256]{0:T(256)S(1)} %bitcast.3) | data formatting | bytes 2048
Async XLA Ops:
  1.3 2.2 %copy-start = (bf16[1,1,128,128,128]{4,3,2,1,0:T(8,128)(2,1)S(1)}, bf16[1,1,128,128,128]{4,3,2,1,0:T(8,128)(2,1)}, u32[]{:S(2)}) copy-start(bf16[1,1,128,128,128]{4,3,2,1,0:T(8,128)(2,1)} %tiles_hbm.1) | copy-start | bytes 12582916
  3.5 0.9 %copy-start.1 = (bf16[256,256]{1,0:T(8,128)(2,1)S(1)}, bf16[256,256]{1,0:T(8,128)(2,1)}, u32[]{:S(2)}) copy-start(bf16[256,256]{1,0:T(8,128)(2,1)} %cot_ref.1) | copy-start | bytes 393220
  4.4 0.8 %copy-start.2 = (bf16[256,128]{1,0:T(8,128)(2,1)S(1)}, bf16[256,128]{1,0:T(8,128)(2,1)}, u32[]{:S(2)}) copy-start(bf16[256,128]{1,0:T(8,128)(2,1)} %feat_ref.1) | copy-start | bytes 196612
  5.2 0.8 %copy-start.3 = (bf16[128,256]{1,0:T(8,128)(2,1)S(1)}, bf16[128,256]{1,0:T(8,128)(2,1)}, u32[]{:S(2)}) copy-start(bf16[128,256]{1,0:T(8,128)(2,1)} %weight_ref.1) | copy-start | bytes 196612
  6.1 0.7 %copy-start.4 = (f32[256]{0:T(256)S(1)}, f32[256]{0:T(256)}, u32[]{:S(2)}) copy-start(f32[256]{0:T(256)} %param.10) | copy-start | bytes 3076
  6.7 0.7 %copy-start.5 = (s32[1,1,2,128]{3,2,1,0:T(2,128)S(1)}, s32[1,1,2,128]{3,2,1,0:T(2,128)}, u32[]{:S(2)}) copy-start(s32[1,1,2,128]{3,2,1,0:T(2,128)} %pos_ref.1) | copy-start | bytes 3076
  7.4 0.7 %copy-start.6 = (s32[64]{0:T(128)S(1)}, s32[64]{0:T(128)}, u32[]{:S(2)}) copy-start(s32[64]{0:T(128)} %perm_ref.1) | copy-start | bytes 772

commit v2 on v1

v2 whole, which is shorter than its diff:
```python
import functools

import jax
import jax.numpy as jnp
from jax import lax
from jax.experimental import pallas as pl
from jax.experimental.pallas import tpu as pltpu
from jax.sharding import PartitionSpec as P

MESH = pl.DeviceIdType.MESH
F32 = jnp.float32
BF16 = jnp.bfloat16
WIRE = jnp.bfloat16
TILE_ROWS = 8
LANES = 128
VMEM_BYTES = 64 * 1024 * 1024


def flip(index, bits):
    place = 1
    while place <= bits:
        if (bits // place) % 2:
            index = index + place - 2 * place * lax.rem(index // place, 2)
        place *= 2
    return index


def kernel(
    row_count,
    col_count,
    feat_hbm,
    weight_hbm,
    bias_hbm,
    cot_hbm,
    tiles_hbm,
    pos_hbm,
    count_hbm,
    perm_hbm,
    hidden_out,
    wgrad_out,
    bgrad_out,
    hidden_ref,
    wgrad_ref,
    bgrad_ref,
    weight_ref,
    bias_ref,
    cot_ref,
    pos_ref,
    count_ref,
    perm_ref,
    tiles,
    dense,
    index_vmem,
    index_smem,
    gathered,
    col_part,
    col_sibling,
    col_buf,
    col_scale,
    row_sums,
    row_send,
    row_buf,
    product,
    prod_send,
    prod_buf,
    grad_send,
    grad_sibling,
    chip_send,
    chip_buf,
    out_buf,
    load_sem,
    store_sem,
    index_sem,
    feat_send_sem,
    feat_recv_sem,
    send_sem,
    recv_sem,
):
    row = lax.axis_index("row")
    col = lax.axis_index("col")
    core = lax.rem(row, 2)
    level = row // 2
    levels = row_count // 2
    chip = level * col_count + col
    chips = levels * col_count
    sibling = row + 1 - 2 * core
    max_tiles = tiles.shape[0] - 1
    tile = tiles.shape[1]
    row_tiles = dense.shape[0] // tile
    col_tiles = dense.shape[1] // tile
    own_rows = hidden_ref.shape[0]
    feat_rows = gathered.shape[1]
    hidden_width = weight_ref.shape[1]
    grad_tiles = out_buf.shape[0]
    core_tiles = grad_tiles // 2
    halves = hidden_width // LANES

    barrier = pltpu.get_barrier_semaphore()

    def greet(step, carry):
        other = lax.rem(chip + step, chips)
        pl.semaphore_signal(
            barrier,
            inc=1,
            device_id=(other // col_count * 2 + core, lax.rem(other, col_count)),
            device_id_type=MESH,
        )
        return carry

    pl.semaphore_signal(barrier, inc=1, device_id=(sibling, col), device_id_type=MESH)
    lax.fori_loop(1, chips, greet, 0)

    loads = [
        pltpu.make_async_copy(source, target, load_sem.at[i])
        for i, (source, target) in enumerate(
            (
                (feat_hbm, gathered.at[row]),
                (pos_hbm.at[0, 0], pos_ref),
                (count_hbm, count_ref),
                (perm_hbm, perm_ref),
                (tiles_hbm.at[0, 0], tiles.at[pl.ds(0, max_tiles)]),
                (weight_hbm, weight_ref),
                (bias_hbm, bias_ref),
                (cot_hbm, cot_ref),
            )
        )
    ]
    for load in loads:
        load.start()
    tiles[max_tiles] = jnp.zeros((tile, tile), BF16)
    for load in loads[1:4]:
        load.wait()

    tile_row = pos_ref[0:1, :]
    tile_col = pos_ref[1:2, :]
    code_row = jnp.zeros((1, max_tiles), jnp.int32)
    for i in range(row_tiles):
        place = perm_ref[row * row_tiles + i] - row * row_tiles
        code_row = jnp.where(tile_row == i, place, code_row)
    code_col = jnp.zeros((1, max_tiles), jnp.int32)
    for j in range(col_tiles):
        place = perm_ref[col * col_tiles + j] - col * col_tiles
        code_col = jnp.where(tile_col == j, place, code_col)
    slot_lane = lax.broadcasted_iota(jnp.int32, (1, max_tiles), 1)
    code = jnp.where(slot_lane < count_ref[0, 0], code_row * col_tiles + code_col, -1)
    code = jnp.transpose(jnp.broadcast_to(code, (LANES, max_tiles)))
    positions = row_tiles * col_tiles
    slot_sub = lax.broadcasted_iota(jnp.int32, (max_tiles, LANES), 0)
    for start in range(0, positions, LANES):
        place = lax.broadcasted_iota(jnp.int32, (max_tiles, LANES), 1) + start
        slot = jnp.min(jnp.where(code == place, slot_sub, max_tiles), axis=0, keepdims=True)
        index_vmem[:, start : start + LANES] = jnp.broadcast_to(slot, (8, LANES))
    index_copy = pltpu.make_async_copy(index_vmem, index_smem, index_sem)
    index_copy.start()

    loads[0].wait()
    pl.semaphore_wait(barrier, chips)

    def feat_copy(source_row, target_row, send_slot):
        return pltpu.make_async_remote_copy(
            src_ref=gathered.at[source_row],
            dst_ref=gathered.at[source_row],
            send_sem=feat_send_sem.at[send_slot],
            recv_sem=feat_recv_sem.at[source_row],
            device_id=(target_row, col),
            device_id_type=MESH,
        )

    for step in range(1, levels):
        feat_copy(row, flip(level, step) * 2 + core, step).start()
    feat_copy(row, sibling, 0).start()

    index_copy.wait()
    loads[4].wait()

    def build(b, carry):
        columns = pl.ds(pl.multiple_of(b * tile, tile), tile)
        total = jnp.zeros((tile, tile), F32)
        for a in range(row_tiles):
            block = tiles[index_smem[0, a * col_tiles + b]]
            dense[a * tile : (a + 1) * tile, columns] = block
            total = total + block.astype(F32)
        col_part[pl.ds(b, 1), :] = jnp.sum(total, axis=0, keepdims=True)
        return carry

    lax.fori_loop(0, col_tiles, build, 0)

    def remote(source, target_ref, target_row, target_col, which):
        return pltpu.make_async_remote_copy(
            src_ref=source,
            dst_ref=target_ref,
            send_sem=send_sem.at[which],
            recv_sem=recv_sem.at[which],
            device_id=(target_row, target_col),
            device_id_type=MESH,
        )

    def wait_all(ref, which):
        copy = remote(ref, ref, sibling, col, which)
        copy.wait_send()
        copy.wait_recv()

    remote(col_part, col_sibling, sibling, col, 0).start()

    def add_rows(k, carry):
        columns = pl.ds(pl.multiple_of(k * feat_rows, feat_rows), feat_rows)
        row_sums[...] += jnp.dot(
            dense[:, columns], jnp.ones((feat_rows, LANES), BF16), preferred_element_type=F32
        )
        return carry

    row_sums[...] = jnp.zeros(row_sums.shape, F32)
    wait_all(col_part, 0)
    col_buf[level] = col_part[...] + col_sibling[...]
    for step in range(1, levels):
        target = flip(level, step) * 2 + core
        remote(col_buf.at[level], col_buf.at[level], target, col, 1).start()

    lax.fori_loop(0, row_count, add_rows, 0)
    for k in range(col_count):
        for at in range(0, own_rows, tile):
            sums = row_sums[k * own_rows + at : k * own_rows + at + tile, :]
            row_send[k, :, at : at + tile] = jnp.transpose(sums)[0:8, :]
    for step in range(1, col_count):
        target = lax.rem(col + step, col_count)
        remote(row_send.at[target], row_buf.at[col], row, target, 2).start()
    row_buf[col] = row_send[col]

    wait_all(col_buf.at[pl.ds(0, levels - 1)], 1)
    col_total = col_buf[0]
    for other in range(1, levels):
        col_total = col_total + col_buf[other]
    col_scale[...] = lax.rsqrt(1.0 + col_total)

    def multiply(source):
        parts = []
        for at in range(0, feat_rows, tile):
            scale = col_scale[pl.ds(source * (feat_rows // tile) + at // tile, 1), :]
            scale = jnp.transpose(jnp.broadcast_to(scale, (tile, tile)))
            parts.append((scale * gathered[source, at : at + tile, :].astype(F32)).astype(BF16))
        columns = pl.ds(pl.multiple_of(source * feat_rows, feat_rows), feat_rows)
        return jnp.dot(
            dense[:, columns], jnp.concatenate(parts, axis=0), preferred_element_type=F32
        )

    product[...] = multiply(row)
    feat_copy(sibling, sibling, 0).wait_recv()
    product[...] += multiply(sibling)
    for step in range(1, levels):
        source = flip(level, step) * 2 + core
        feat_copy(source, sibling, 0).wait_recv()
        feat_copy(source, sibling, levels + step - 1).start()
        product[...] += multiply(source)
    for step in range(1, levels):
        source = flip(level, step) * 2 + 1 - core
        feat_copy(source, sibling, 0).wait_recv()
        product[...] += multiply(source)

    def piece(owner):
        return product[pl.ds(pl.multiple_of(owner * own_rows, own_rows), own_rows), :]

    for step in range(1, col_count):
        target = lax.rem(col + step, col_count)
        prod_send[step - 1] = piece(target).astype(WIRE)
        remote(prod_send.at[step - 1], prod_buf.at[col], row, target, 3).start()

    wait_all(row_buf.at[pl.ds(0, col_count - 1)], 2)
    row_total = row_buf[0]
    for c in range(1, col_count):
        row_total = row_total + row_buf[c]
    row_scale = lax.rsqrt(1.0 + row_total)
    row_scale = jnp.concatenate(
        [
            jnp.transpose(
                jnp.broadcast_to(row_scale[0:1, at : at + tile], (LANES, tile))
            )
            for at in range(0, own_rows, tile)
        ],
        axis=0,
    )
    prod_buf[col] = jnp.zeros(prod_buf.shape[1:], WIRE)
    for load in loads[5:]:
        load.wait()
    wait_all(prod_buf.at[pl.ds(0, col_count - 1)], 3)
    summed = piece(col)
    for c in range(col_count):
        summed = summed + prod_buf[c].astype(F32)

    aggregated = (row_scale * summed).astype(BF16)
    preact = jnp.dot(aggregated, weight_ref[...], preferred_element_type=F32) + bias_ref[...]
    logistic = jax.nn.sigmoid(preact)
    preact_grad = (
        cot_ref[...].astype(F32) * logistic * (1.0 + preact * (1.0 - logistic))
    ).astype(BF16)
    weight_part = lax.dot_general(
        aggregated, preact_grad, (((0,), (0,)), ((), ())), preferred_element_type=F32
    )
    bias_part = jnp.sum(preact_grad.astype(F32), axis=0, keepdims=True)

    bias_rows = jnp.concatenate(
        [bias_part[:, h * LANES : (h + 1) * LANES] for h in range(halves)]
        + [jnp.zeros((TILE_ROWS - halves, LANES), F32)],
        axis=0,
    )
    for t in range(grad_tiles):
        i, h = t // halves, t % halves
        part = weight_part[i * TILE_ROWS : (i + 1) * TILE_ROWS, h * LANES : (h + 1) * LANES]
        grad_send[t] = jnp.concatenate([part, bias_rows], axis=0)
    mine = pl.ds(pl.multiple_of(core * core_tiles, core_tiles), core_tiles)
    theirs = pl.ds(pl.multiple_of((1 - core) * core_tiles, core_tiles), core_tiles)
    remote(grad_send.at[theirs], grad_sibling, sibling, col, 4).start()
    hidden_ref[...] = (preact * logistic).astype(BF16)
    hidden_store = pltpu.make_async_copy(hidden_ref, hidden_out, store_sem.at[0])
    hidden_store.start()
    wait_all(grad_sibling, 4)
    chip_send[...] = (grad_send[mine] + grad_sibling[...]).astype(BF16)

    def send_part(step, carry):
        other = lax.rem(chip + step, chips)
        remote(
            chip_send.at[lax.rem(other, core_tiles)],
            chip_buf.at[chip],
            other // col_count * 2 + core,
            lax.rem(other, col_count),
            5,
        ).start()
        return carry

    lax.fori_loop(1, chips, send_part, 0)
    own = lax.rem(chip, core_tiles)
    chip_buf[chip] = chip_send[own]
    wait_all(chip_buf.at[pl.ds(0, chips - 1)], 5)

    def add_part(d, total):
        return total + chip_buf[d].astype(F32)

    total = lax.fori_loop(
        0, chips, add_part, jnp.zeros((2 * TILE_ROWS, LANES), F32), unroll=min(chips, 16)
    )
    inverse_root = lax.rsqrt(F32(own_rows * row_count * col_count))
    total = total * inverse_root
    slot = core * core_tiles + own
    out_buf[slot] = total[0:TILE_ROWS]
    first = chip - own

    def send_total(step, carry):
        other = first + lax.rem(own + step, core_tiles)
        remote(
            out_buf.at[slot],
            out_buf.at[slot],
            other // col_count * 2 + core,
            lax.rem(other, col_count),
            6,
        ).start()
        return carry

    lax.fori_loop(1, core_tiles, send_total, 0)
    for h in range(halves):
        bgrad_ref[:, h * LANES : (h + 1) * LANES] = total[TILE_ROWS + h : TILE_ROWS + h + 1]
    bgrad_store = pltpu.make_async_copy(bgrad_ref, bgrad_out, store_sem.at[1])
    bgrad_store.start()
    for step in range(2 * levels - 1):
        feat_copy(row, sibling, step).wait_send()
    hidden_store.wait()
    bgrad_store.wait()
    wait_all(out_buf.at[pl.ds(0, core_tiles - 1)], 6)
    remote(out_buf.at[mine], out_buf.at[mine], sibling, col, 7).start()
    wait_all(out_buf.at[pl.ds(0, core_tiles)], 7)
    for t in range(grad_tiles):
        i, h = t // halves, t % halves
        wgrad_ref[i * TILE_ROWS : (i + 1) * TILE_ROWS, h * LANES : (h + 1) * LANES] = out_buf[t]
    wgrad_store = pltpu.make_async_copy(wgrad_ref, wgrad_out, store_sem.at[2])
    wgrad_store.start()
    wgrad_store.wait()


def write_out(*refs):
    count = len(refs) // 2
    sems = refs[-1]
    copies = [
        pltpu.make_async_copy(refs[i], refs[count + i], sems.at[i]) for i in range(count)
    ]
    for copy in copies:
        copy.start()
    for copy in copies:
        copy.wait()


def solution(mesh):
    row_count = mesh.shape["row"]
    col_count = mesh.shape["col"]
    device_count = row_count * col_count

    def body(features, weight, bias, cotangent, tile_values, tile_pos, tile_count, block_perm):
        max_tiles, tile = tile_values.shape[2], tile_values.shape[3]
        row_tiles = block_perm.shape[0] // row_count
        col_tiles = block_perm.shape[0] // col_count
        feat_rows, feat_width = features.shape
        own_rows, hidden_width = cotangent.shape
        grad_tiles = feat_width * hidden_width // (TILE_ROWS * LANES)
        hbm = pl.BlockSpec(memory_space=pl.ANY)
        shapes = (
            jax.ShapeDtypeStruct((own_rows, hidden_width), BF16),
            jax.ShapeDtypeStruct((feat_width, hidden_width), F32),
            jax.ShapeDtypeStruct((1, hidden_width), F32),
        )
        results = pl.pallas_call(
            functools.partial(kernel, row_count, col_count),
            out_shape=shapes,
            in_specs=[hbm] * 8,
            out_specs=(hbm, hbm, hbm),
            scratch_shapes=[
                pltpu.VMEM((own_rows, hidden_width), BF16),
                pltpu.VMEM((feat_width, hidden_width), F32),
                pltpu.VMEM((1, hidden_width), F32),
                pltpu.VMEM(weight.shape, BF16),
                pltpu.VMEM((1, hidden_width), F32),
                pltpu.VMEM(cotangent.shape, BF16),
                pltpu.VMEM(tile_pos.shape[2:], jnp.int32),
                pltpu.SMEM(tile_count.shape, jnp.int32),
                pltpu.SMEM(block_perm.shape, jnp.int32),
                pltpu.VMEM((max_tiles + 1, tile, tile), BF16),
                pltpu.VMEM((row_tiles * tile, col_tiles * tile), BF16),
                pltpu.VMEM((8, row_tiles * col_tiles), jnp.int32),
                pltpu.SMEM((8, row_tiles * col_tiles), jnp.int32),
                pltpu.VMEM((row_count, feat_rows, feat_width), BF16),
                pltpu.VMEM((col_tiles, tile), F32),
                pltpu.VMEM((col_tiles, tile), F32),
                pltpu.VMEM((row_count // 2, col_tiles, tile), F32),
                pltpu.VMEM((col_tiles, tile), F32),
                pltpu.VMEM((row_tiles * tile, LANES), F32),
                pltpu.VMEM((col_count, 8, own_rows), F32),
                pltpu.VMEM((col_count, 8, own_rows), F32),
                pltpu.VMEM((row_tiles * tile, feat_width), F32),
                pltpu.VMEM((col_count - 1, own_rows, feat_width), WIRE),
                pltpu.VMEM((col_count, own_rows, feat_width), WIRE),
                pltpu.VMEM((grad_tiles, 2 * TILE_ROWS, LANES), F32),
                pltpu.VMEM((grad_tiles // 2, 2 * TILE_ROWS, LANES), F32),
                pltpu.VMEM((grad_tiles // 2, 2 * TILE_ROWS, LANES), BF16),
                pltpu.VMEM((device_count // 2, 2 * TILE_ROWS, LANES), BF16),
                pltpu.VMEM((grad_tiles, TILE_ROWS, LANES), F32),
                pltpu.SemaphoreType.DMA((8,)),
                pltpu.SemaphoreType.DMA((3,)),
                pltpu.SemaphoreType.DMA,
                pltpu.SemaphoreType.DMA((row_count,)),
                pltpu.SemaphoreType.DMA((row_count,)),
                pltpu.SemaphoreType.DMA((8,)),
                pltpu.SemaphoreType.DMA((8,)),
            ],
            compiler_params=pltpu.CompilerParams(
                collective_id=0, has_side_effects=True, vmem_limit_bytes=VMEM_BYTES
            ),
        )(
            features,
            weight,
            bias.reshape(1, hidden_width),
            cotangent,
            tile_values,
            tile_pos,
            tile_count,
            block_perm,
        )
        hidden, weight_grad, bias_grad = pl.pallas_call(
            write_out,
            out_shape=shapes,
            in_specs=[hbm] * 3,
            out_specs=(hbm, hbm, hbm),
            scratch_shapes=[pltpu.SemaphoreType.DMA((3,))],
            compiler_params=pltpu.CompilerParams(vmem_limit_bytes=VMEM_BYTES),
        )(*results)
        return hidden, weight_grad, bias_grad.reshape(hidden_width)

    return jax.shard_map(
        body,
        mesh=mesh,
        in_specs=(
            P(("col", "row"), None),
            P(),
            P(),
            P(("row", "col"), None),
            P("row", "col", None, None, None),
            P("row", "col", None, None),
            P("row", "col"),
            P(),
        ),
        out_specs=(P(("row", "col"), None), P(), P()),
        check_vma=False,
    )
```

time: 47.3 us -> 45.6 us (0.964)
  local copies, waits for them, and re-layouts: 8.65 us -> 0 us
  Pallas kernels: 36.9 us -> 44.2 us
    pallas_call x0 -> x1, Pallas kernels: none -> 9.1 us  [body(): pl.pallas_call(write_out, out_shape=shapes, in_specs=[hbm] * 3, out_specs...]
    unnamed x17 -> x0, local copies, waits for them, and re-layouts: 8.65 us -> none
    pallas_call x1, Pallas kernels: 36.9 us -> 35.1 us  [body(): pl.pallas_call(functools.partial(kernel, row_count, col_count), out_shape...]
where the time goes in v2:
time: 45.6 us; the launch traced here: 45.4 us
  Pallas kernels  44.2 us (97%)
  between operations  1.29 us (3%)
    pallas_call x1, Pallas kernels, body(): pl.pallas_call(functools.partial(kernel, row_count, col_count), out_shape...  35.1 us
    pallas_call x1, Pallas kernels, body(): pl.pallas_call(write_out, out_shape=shapes, in_specs=[hbm] * 3, out_specs...  9.1 us

profile of v2, /device:TPU:0, one launch (start us, length us, event | category | flops | bytes accessed | tf_op | source)
XLA Modules:
  0.0 45.4 jit_solution(10733663434716800002)
XLA Ops:
  1.3 35.1 %shard_map.103 = (bf16[256,256]{1,0:T(8,128)(2,1)}, f32[128,256]{1,0:T(8,128)}, f32[1,256]{1,0:T(1,128)}) custom-call(bf16[256,128]{1,0:T(8,128)(2,1)} %feat_hbm.1, bf16[128,256]{1,0:T(8,128)(2,1)} %weight_hbm.1, f32[1,256]{1,0:T(1,128)} %bitcast.2, bf16[256,256]{1,0:T(8,128)(2,1)} %cot_hbm.1, bf16[1,1,128,128,128]{4,3,2,1,0:T(8,128)(2,1)} %tiles_hbm.1, ...), custom_call_target="tpu_custom_call" | custom-call | tf_op jit(solution)/shard_map/pallas_call | solution.py:407
  36.3 9.1 %shard_map.104 = (bf16[256,256]{1,0:T(8,128)(2,1)}, f32[128,256]{1,0:T(8,128)}, f32[1,256]{1,0:T(1,128)}) custom-call(bf16[256,256]{1,0:T(8,128)(2,1)} %get-tuple-element.9.refs_0_, f32[128,256]{1,0:T(8,128)} %get-tuple-element.10.refs_1_, f32[1,256]{1,0:T(1,128)} %get-tuple-element.11.refs_2_), custom_call_target="tpu_custom_call" | custom-call | tf_op jit(solution)/shard_map/pallas_call | solution.py:463

commit v3 on v2

--- a/solution.py
+++ b/solution.py
@@ -60,7 +60,7 @@
     row_sums,
     row_send,
     row_buf,
-    product,
+    scaled,
     prod_send,
     prod_buf,
     grad_send,
@@ -89,26 +89,11 @@
     row_tiles = dense.shape[0] // tile
     col_tiles = dense.shape[1] // tile
     own_rows = hidden_ref.shape[0]
-    feat_rows = gathered.shape[1]
+    feat_rows, feat_width = gathered.shape[1:]
     hidden_width = weight_ref.shape[1]
     grad_tiles = out_buf.shape[0]
     core_tiles = grad_tiles // 2
     halves = hidden_width // LANES
-
-    barrier = pltpu.get_barrier_semaphore()
-
-    def greet(step, carry):
-        other = lax.rem(chip + step, chips)
-        pl.semaphore_signal(
-            barrier,
-            inc=1,
-            device_id=(other // col_count * 2 + core, lax.rem(other, col_count)),
-            device_id_type=MESH,
-        )
-        return carry
-
-    pl.semaphore_signal(barrier, inc=1, device_id=(sibling, col), device_id_type=MESH)
-    lax.fori_loop(1, chips, greet, 0)
 
     loads = [
         pltpu.make_async_copy(source, target, load_sem.at[i])
@@ -127,6 +112,21 @@
     ]
     for load in loads:
         load.start()
+    barrier = pltpu.get_barrier_semaphore()
+
+    def greet(step, carry):
+        other = lax.rem(chip + step, chips)
+        pl.semaphore_signal(
+            barrier,
+            inc=1,
+            device_id=(other // col_count * 2 + core, lax.rem(other, col_count)),
+            device_id_type=MESH,
+        )
+        return carry
+
+    pl.semaphore_signal(barrier, inc=1, device_id=(sibling, col), device_id_type=MESH)
+    lax.fori_loop(1, chips, greet, 0)
+
     tiles[max_tiles] = jnp.zeros((tile, tile), BF16)
     for load in loads[1:4]:
         load.wait()
@@ -202,10 +202,12 @@
 
     remote(col_part, col_sibling, sibling, col, 0).start()
 
+    depth = 2 * feat_rows
+
     def add_rows(k, carry):
-        columns = pl.ds(pl.multiple_of(k * feat_rows, feat_rows), feat_rows)
+        columns = pl.ds(pl.multiple_of(k * depth, depth), depth)
         row_sums[...] += jnp.dot(
-            dense[:, columns], jnp.ones((feat_rows, LANES), BF16), preferred_element_type=F32
+            dense[:, columns], jnp.ones((depth, LANES), BF16), preferred_element_type=F32
         )
         return carry
 
@@ -216,7 +218,7 @@
         target = flip(level, step) * 2 + core
         remote(col_buf.at[level], col_buf.at[level], target, col, 1).start()
 
-    lax.fori_loop(0, row_count, add_rows, 0)
+    lax.fori_loop(0, row_count // 2, add_rows, 0)
     for k in range(col_count):
         for at in range(0, own_rows, tile):
             sums = row_sums[k * own_rows + at : k * own_rows + at + tile, :]
@@ -226,43 +228,46 @@
         remote(row_send.at[target], row_buf.at[col], row, target, 2).start()
     row_buf[col] = row_send[col]
 
+    for step in range(1, levels):
+        source = flip(level, step) * 2 + core
+        feat_copy(source, sibling, 0).wait_recv()
+        feat_copy(source, sibling, levels + step - 1).start()
+
     wait_all(col_buf.at[pl.ds(0, levels - 1)], 1)
     col_total = col_buf[0]
     for other in range(1, levels):
         col_total = col_total + col_buf[other]
-    col_scale[...] = lax.rsqrt(1.0 + col_total)
-
-    def multiply(source):
-        parts = []
-        for at in range(0, feat_rows, tile):
-            scale = col_scale[pl.ds(source * (feat_rows // tile) + at // tile, 1), :]
-            scale = jnp.transpose(jnp.broadcast_to(scale, (tile, tile)))
-            parts.append((scale * gathered[source, at : at + tile, :].astype(F32)).astype(BF16))
-        columns = pl.ds(pl.multiple_of(source * feat_rows, feat_rows), feat_rows)
-        return jnp.dot(
-            dense[:, columns], jnp.concatenate(parts, axis=0), preferred_element_type=F32
-        )
-
-    product[...] = multiply(row)
+    scale = jnp.concatenate(
+        [lax.rsqrt(1.0 + col_total), jnp.zeros((LANES - col_tiles, tile), F32)], axis=0
+    )
+    scale = jnp.transpose(scale)
+    for j in range(col_tiles):
+        col_scale[j] = jnp.broadcast_to(scale[:, j : j + 1], (tile, feat_width))
+
+    def scale_rows(source):
+        for i in range(feat_rows // tile):
+            j = source * (feat_rows // tile) + i
+            block = gathered[source, i * tile : (i + 1) * tile, :].astype(F32)
+            rows = pl.ds(pl.multiple_of(j * tile, tile), tile)
+            scaled[rows, :] = (col_scale[j] * block).astype(BF16)
+
+    for step in range(levels):
+        scale_rows(flip(level, step) * 2 + core)
     feat_copy(sibling, sibling, 0).wait_recv()
-    product[...] += multiply(sibling)
     for step in range(1, levels):
-        source = flip(level, step) * 2 + core
-        feat_copy(source, sibling, 0).wait_recv()
-        feat_copy(source, sibling, levels + step - 1).start()
-        product[...] += multiply(source)
-    for step in range(1, levels):
-        source = flip(level, step) * 2 + 1 - core
-        feat_copy(source, sibling, 0).wait_recv()
-        product[...] += multiply(source)
+        feat_copy(flip(level, step) * 2 + 1 - core, sibling, 0).wait_recv()
+    for step in range(levels):
+        scale_rows(flip(level, step) * 2 + 1 - core)
 
     def piece(owner):
-        return product[pl.ds(pl.multiple_of(owner * own_rows, own_rows), own_rows), :]
+        rows = pl.ds(pl.multiple_of(owner * own_rows, own_rows), own_rows)
+        return jnp.dot(dense[rows, :], scaled[...], preferred_element_type=F32)
 
     for step in range(1, col_count):
         target = lax.rem(col + step, col_count)
         prod_send[step - 1] = piece(target).astype(WIRE)
         remote(prod_send.at[step - 1], prod_buf.at[col], row, target, 3).start()
+    summed = piece(col)
 
     wait_all(row_buf.at[pl.ds(0, col_count - 1)], 2)
     row_total = row_buf[0]
@@ -282,7 +287,6 @@
     for load in loads[5:]:
         load.wait()
     wait_all(prod_buf.at[pl.ds(0, col_count - 1)], 3)
-    summed = piece(col)
     for c in range(col_count):
         summed = summed + prod_buf[c].astype(F32)
 
@@ -375,15 +379,16 @@
 
 
 def write_out(*refs):
-    count = len(refs) // 2
-    sems = refs[-1]
-    copies = [
-        pltpu.make_async_copy(refs[i], refs[count + i], sems.at[i]) for i in range(count)
-    ]
-    for copy in copies:
-        copy.start()
-    for copy in copies:
-        copy.wait()
+    ins, outs, held, sems = refs[0:3], refs[3:6], refs[6:9], refs[9]
+    loads = [pltpu.make_async_copy(ins[i], held[i], sems.at[0, i]) for i in range(3)]
+    stores = [pltpu.make_async_copy(held[i], outs[i], sems.at[1, i]) for i in range(3)]
+    for load in loads:
+        load.start()
+    for load, store in zip(loads, stores):
+        load.wait()
+        store.start()
+    for store in stores:
+        store.wait()
 
 
 def solution(mesh):
@@ -427,11 +432,11 @@
                 pltpu.VMEM((col_tiles, tile), F32),
                 pltpu.VMEM((col_tiles, tile), F32),
                 pltpu.VMEM((row_count // 2, col_tiles, tile), F32),
-                pltpu.VMEM((col_tiles, tile), F32),
+                pltpu.VMEM((col_tiles, tile, feat_width), F32),
                 pltpu.VMEM((row_tiles * tile, LANES), F32),
                 pltpu.VMEM((col_count, 8, own_rows), F32),
                 pltpu.VMEM((col_count, 8, own_rows), F32),
-                pltpu.VMEM((row_tiles * tile, feat_width), F32),
+                pltpu.VMEM((col_tiles * tile, feat_width), BF16),
                 pltpu.VMEM((col_count - 1, own_rows, feat_width), WIRE),
                 pltpu.VMEM((col_count, own_rows, feat_width), WIRE),
                 pltpu.VMEM((grad_tiles, 2 * TILE_ROWS, LANES), F32),
@@ -465,7 +470,10 @@
             out_shape=shapes,
             in_specs=[hbm] * 3,
             out_specs=(hbm, hbm, hbm),
-            scratch_shapes=[pltpu.SemaphoreType.DMA((3,))],
+            scratch_shapes=[
+                *(pltpu.VMEM(shape.shape, shape.dtype) for shape in shapes),
+                pltpu.SemaphoreType.DMA((2, 3)),
+            ],
             compiler_params=pltpu.CompilerParams(vmem_limit_bytes=VMEM_BYTES),
         )(*results)
         return hidden, weight_grad, bias_grad.reshape(hidden_width)

time: 45.6 us -> 36.2 us (0.79)
  Pallas kernels: 44.2 us -> 34.7 us
    pallas_call x1, Pallas kernels: 9.1 us -> 1.68 us  [body(): pl.pallas_call(write_out, out_shape=shapes, in_specs=[hbm] * 3, out_specs...]
    pallas_call x1, Pallas kernels: 35.1 us -> 33.1 us  [body(): pl.pallas_call(functools.partial(kernel, row_count, col_count), out_shape...]
where the time goes in v3:
time: 36.2 us; the launch traced here: 36 us
  Pallas kernels  34.7 us (96%)
  between operations  1.29 us (4%)
    pallas_call x1, Pallas kernels, body(): pl.pallas_call(functools.partial(kernel, row_count, col_count), out_shape...  33.1 us
    pallas_call x1, Pallas kernels, body(): pl.pallas_call(write_out, out_shape=shapes, in_specs=[hbm] * 3, out_specs...  1.68 us

profile of v3, /device:TPU:0, one launch (start us, length us, event | category | flops | bytes accessed | tf_op | source)
XLA Modules:
  0.0 36.0 jit_solution(16730221163646994453)
XLA Ops:
  1.3 33.1 %shard_map.103 = (bf16[256,256]{1,0:T(8,128)(2,1)}, f32[128,256]{1,0:T(8,128)}, f32[1,256]{1,0:T(1,128)}) custom-call(bf16[256,128]{1,0:T(8,128)(2,1)} %feat_hbm.1, bf16[128,256]{1,0:T(8,128)(2,1)} %weight_hbm.1, f32[1,256]{1,0:T(1,128)} %bitcast.2, bf16[256,256]{1,0:T(8,128)(2,1)} %cot_hbm.1, bf16[1,1,128,128,128]{4,3,2,1,0:T(8,128)(2,1)} %tiles_hbm.1, ...), custom_call_target="tpu_custom_call" | custom-call | tf_op jit(solution)/shard_map/pallas_call | solution.py:412
  34.4 1.7 %shard_map.104 = (bf16[256,256]{1,0:T(8,128)(2,1)}, f32[128,256]{1,0:T(8,128)}, f32[1,256]{1,0:T(1,128)}) custom-call(bf16[256,256]{1,0:T(8,128)(2,1)} %get-tuple-element.9.refs_0_, f32[128,256]{1,0:T(8,128)} %get-tuple-element.10.refs_1_, f32[1,256]{1,0:T(1,128)} %get-tuple-element.11.refs_2_), custom_call_target="tpu_custom_call" | custom-call | tf_op jit(solution)/shard_map/pallas_call | solution.py:468

commit v4 on v3

--- a/solution.py
+++ b/solution.py
@@ -13,7 +13,7 @@
 WIRE = jnp.bfloat16
 TILE_ROWS = 8
 LANES = 128
-VMEM_BYTES = 64 * 1024 * 1024
+VMEM_BYTES = 48 * 1024 * 1024
 
 
 def flip(index, bits):
@@ -36,9 +36,6 @@
     pos_hbm,
     count_hbm,
     perm_hbm,
-    hidden_out,
-    wgrad_out,
-    bgrad_out,
     hidden_ref,
     wgrad_ref,
     bgrad_ref,
@@ -69,7 +66,6 @@
     chip_buf,
     out_buf,
     load_sem,
-    store_sem,
     index_sem,
     feat_send_sem,
     feat_recv_sem,
@@ -84,6 +80,11 @@
     chip = level * col_count + col
     chips = levels * col_count
     sibling = row + 1 - 2 * core
+    level_flips = [flip(level, step) for step in range(levels)]
+    col_flips = [flip(col, step) for step in range(col_count)]
+    others = [
+        (level_flips[step // col_count], col_flips[step % col_count]) for step in range(1, chips)
+    ]
     max_tiles = tiles.shape[0] - 1
     tile = tiles.shape[1]
     row_tiles = dense.shape[0] // tile
@@ -114,19 +115,14 @@
         load.start()
     barrier = pltpu.get_barrier_semaphore()
 
-    def greet(step, carry):
-        other = lax.rem(chip + step, chips)
+    pl.semaphore_signal(barrier, inc=1, device_id=(sibling, col), device_id_type=MESH)
+    for other_level, other_col in others:
         pl.semaphore_signal(
             barrier,
             inc=1,
-            device_id=(other // col_count * 2 + core, lax.rem(other, col_count)),
+            device_id=(other_level * 2 + core, other_col),
             device_id_type=MESH,
         )
-        return carry
-
-    pl.semaphore_signal(barrier, inc=1, device_id=(sibling, col), device_id_type=MESH)
-    lax.fori_loop(1, chips, greet, 0)
-
     tiles[max_tiles] = jnp.zeros((tile, tile), BF16)
     for load in loads[1:4]:
         load.wait()
@@ -167,7 +163,7 @@
         )
 
     for step in range(1, levels):
-        feat_copy(row, flip(level, step) * 2 + core, step).start()
+        feat_copy(row, level_flips[step] * 2 + core, step).start()
     feat_copy(row, sibling, 0).start()
 
     index_copy.wait()
@@ -215,7 +211,7 @@
     wait_all(col_part, 0)
     col_buf[level] = col_part[...] + col_sibling[...]
     for step in range(1, levels):
-        target = flip(level, step) * 2 + core
+        target = level_flips[step] * 2 + core
         remote(col_buf.at[level], col_buf.at[level], target, col, 1).start()
 
     lax.fori_loop(0, row_count // 2, add_rows, 0)
@@ -224,12 +220,12 @@
             sums = row_sums[k * own_rows + at : k * own_rows + at + tile, :]
             row_send[k, :, at : at + tile] = jnp.transpose(sums)[0:8, :]
     for step in range(1, col_count):
-        target = lax.rem(col + step, col_count)
+        target = col_flips[step]
         remote(row_send.at[target], row_buf.at[col], row, target, 2).start()
     row_buf[col] = row_send[col]
 
     for step in range(1, levels):
-        source = flip(level, step) * 2 + core
+        source = level_flips[step] * 2 + core
         feat_copy(source, sibling, 0).wait_recv()
         feat_copy(source, sibling, levels + step - 1).start()
 
@@ -252,19 +248,19 @@
             scaled[rows, :] = (col_scale[j] * block).astype(BF16)
 
     for step in range(levels):
-        scale_rows(flip(level, step) * 2 + core)
+        scale_rows(level_flips[step] * 2 + core)
     feat_copy(sibling, sibling, 0).wait_recv()
     for step in range(1, levels):
-        feat_copy(flip(level, step) * 2 + 1 - core, sibling, 0).wait_recv()
+        feat_copy(level_flips[step] * 2 + 1 - core, sibling, 0).wait_recv()
     for step in range(levels):
-        scale_rows(flip(level, step) * 2 + 1 - core)
+        scale_rows(level_flips[step] * 2 + 1 - core)
 
     def piece(owner):
         rows = pl.ds(pl.multiple_of(owner * own_rows, own_rows), own_rows)
         return jnp.dot(dense[rows, :], scaled[...], preferred_element_type=F32)
 
-    for step in range(1, col_count):
-        target = lax.rem(col + step, col_count)
+    for step in reversed(range(1, col_count)):
+        target = col_flips[step]
         prod_send[step - 1] = piece(target).astype(WIRE)
         remote(prod_send.at[step - 1], prod_buf.at[col], row, target, 3).start()
     summed = piece(col)
@@ -314,23 +310,18 @@
     theirs = pl.ds(pl.multiple_of((1 - core) * core_tiles, core_tiles), core_tiles)
     remote(grad_send.at[theirs], grad_sibling, sibling, col, 4).start()
     hidden_ref[...] = (preact * logistic).astype(BF16)
-    hidden_store = pltpu.make_async_copy(hidden_ref, hidden_out, store_sem.at[0])
-    hidden_store.start()
     wait_all(grad_sibling, 4)
     chip_send[...] = (grad_send[mine] + grad_sibling[...]).astype(BF16)
 
-    def send_part(step, carry):
-        other = lax.rem(chip + step, chips)
+    for other_level, other_col in others:
+        other = other_level * col_count + other_col
         remote(
             chip_send.at[lax.rem(other, core_tiles)],
             chip_buf.at[chip],
-            other // col_count * 2 + core,
-            lax.rem(other, col_count),
+            other_level * 2 + core,
+            other_col,
             5,
         ).start()
-        return carry
-
-    lax.fori_loop(1, chips, send_part, 0)
     own = lax.rem(chip, core_tiles)
     chip_buf[chip] = chip_send[own]
     wait_all(chip_buf.at[pl.ds(0, chips - 1)], 5)
@@ -345,47 +336,26 @@
     total = total * inverse_root
     slot = core * core_tiles + own
     out_buf[slot] = total[0:TILE_ROWS]
-    first = chip - own
-
-    def send_total(step, carry):
-        other = first + lax.rem(own + step, core_tiles)
+    for other_level, other_col in others[: core_tiles - 1]:
         remote(
-            out_buf.at[slot],
-            out_buf.at[slot],
-            other // col_count * 2 + core,
-            lax.rem(other, col_count),
-            6,
+            out_buf.at[slot], out_buf.at[slot], other_level * 2 + core, other_col, 6
         ).start()
-        return carry
-
-    lax.fori_loop(1, core_tiles, send_total, 0)
     for h in range(halves):
         bgrad_ref[:, h * LANES : (h + 1) * LANES] = total[TILE_ROWS + h : TILE_ROWS + h + 1]
-    bgrad_store = pltpu.make_async_copy(bgrad_ref, bgrad_out, store_sem.at[1])
-    bgrad_store.start()
     for step in range(2 * levels - 1):
         feat_copy(row, sibling, step).wait_send()
-    hidden_store.wait()
-    bgrad_store.wait()
     wait_all(out_buf.at[pl.ds(0, core_tiles - 1)], 6)
     remote(out_buf.at[mine], out_buf.at[mine], sibling, col, 7).start()
     wait_all(out_buf.at[pl.ds(0, core_tiles)], 7)
     for t in range(grad_tiles):
         i, h = t // halves, t % halves
         wgrad_ref[i * TILE_ROWS : (i + 1) * TILE_ROWS, h * LANES : (h + 1) * LANES] = out_buf[t]
-    wgrad_store = pltpu.make_async_copy(wgrad_ref, wgrad_out, store_sem.at[2])
-    wgrad_store.start()
-    wgrad_store.wait()
 
 
 def write_out(*refs):
-    ins, outs, held, sems = refs[0:3], refs[3:6], refs[6:9], refs[9]
-    loads = [pltpu.make_async_copy(ins[i], held[i], sems.at[0, i]) for i in range(3)]
-    stores = [pltpu.make_async_copy(held[i], outs[i], sems.at[1, i]) for i in range(3)]
-    for load in loads:
-        load.start()
-    for load, store in zip(loads, stores):
-        load.wait()
+    ins, outs, sems = refs[0:3], refs[3:6], refs[6]
+    stores = [pltpu.make_async_copy(ins[i], outs[i], sems.at[i]) for i in range(3)]
+    for store in stores:
         store.start()
     for store in stores:
         store.wait()
@@ -404,6 +374,7 @@
         own_rows, hidden_width = cotangent.shape
         grad_tiles = feat_width * hidden_width // (TILE_ROWS * LANES)
         hbm = pl.BlockSpec(memory_space=pl.ANY)
+        vmem = pl.BlockSpec(memory_space=pltpu.VMEM)
         shapes = (
             jax.ShapeDtypeStruct((own_rows, hidden_width), BF16),
             jax.ShapeDtypeStruct((feat_width, hidden_width), F32),
@@ -413,11 +384,8 @@
             functools.partial(kernel, row_count, col_count),
             out_shape=shapes,
             in_specs=[hbm] * 8,
-            out_specs=(hbm, hbm, hbm),
+            out_specs=(vmem, vmem, vmem),
             scratch_shapes=[
-                pltpu.VMEM((own_rows, hidden_width), BF16),
-                pltpu.VMEM((feat_width, hidden_width), F32),
-                pltpu.VMEM((1, hidden_width), F32),
                 pltpu.VMEM(weight.shape, BF16),
                 pltpu.VMEM((1, hidden_width), F32),
                 pltpu.VMEM(cotangent.shape, BF16),
@@ -445,7 +413,6 @@
                 pltpu.VMEM((device_count // 2, 2 * TILE_ROWS, LANES), BF16),
                 pltpu.VMEM((grad_tiles, TILE_ROWS, LANES), F32),
                 pltpu.SemaphoreType.DMA((8,)),
-                pltpu.SemaphoreType.DMA((3,)),
                 pltpu.SemaphoreType.DMA,
                 pltpu.SemaphoreType.DMA((row_count,)),
                 pltpu.SemaphoreType.DMA((row_count,)),
@@ -456,25 +423,21 @@
                 collective_id=0, has_side_effects=True, vmem_limit_bytes=VMEM_BYTES
             ),
         )(
-            features,
-            weight,
-            bias.reshape(1, hidden_width),
-            cotangent,
-            tile_values,
-            tile_pos,
+            *(
+                pltpu.with_memory_space_constraint(operand, pltpu.HBM)
+                for operand in (features, weight, bias.reshape(1, hidden_width), cotangent)
+            ),
+            pltpu.with_memory_space_constraint(tile_values, pltpu.HBM),
+            pltpu.with_memory_space_constraint(tile_pos, pltpu.HBM),
             tile_count,
-            block_perm,
+            pltpu.with_memory_space_constraint(block_perm, pltpu.HBM),
         )
         hidden, weight_grad, bias_grad = pl.pallas_call(
             write_out,
             out_shape=shapes,
-            in_specs=[hbm] * 3,
+            in_specs=[vmem] * 3,
             out_specs=(hbm, hbm, hbm),
-            scratch_shapes=[
-                *(pltpu.VMEM(shape.shape, shape.dtype) for shape in shapes),
-                pltpu.SemaphoreType.DMA((2, 3)),
-            ],
-            compiler_params=pltpu.CompilerParams(vmem_limit_bytes=VMEM_BYTES),
+            scratch_shapes=[pltpu.SemaphoreType.DMA((3,))],
         )(*results)
         return hidden, weight_grad, bias_grad.reshape(hidden_width)
 

time: 36.2 us -> 37.6 us (1.039)
  local copies, waits for them, and re-layouts: 0 us -> 1.88 us
  Pallas kernels: 34.7 us -> 34.3 us
    unnamed x0 -> x6, local copies, waits for them, and re-layouts: none -> 1.88 us
    pallas_call x1, Pallas kernels: 33.1 us -> 32.6 us  [body(): pl.pallas_call(functools.partial(kernel, row_count, col_count), out_shape...]
where the time goes in v4:
time: 37.6 us; the launch traced here: 37.4 us
  Pallas kernels  34.3 us (91%)
  local copies, waits for them, and re-layouts  1.88 us (5%)
  between operations  1.3 us (3%)
    pallas_call x1, Pallas kernels, body(): pl.pallas_call(functools.partial(kernel, row_count, col_count), out_shape...  32.6 us
    unnamed x6, local copies, waits for them, and re-layouts  1.88 us
    pallas_call x1, Pallas kernels, body(): pl.pallas_call(write_out, out_shape=shapes, in_specs=[vmem] * 3, out_spec...  1.69 us

profile of v4, /device:TPU:0, one launch (start us, length us, event | category | flops | bytes accessed | tf_op | source)
XLA Modules:
  0.0 37.4 jit_solution(4564482899698728915)
XLA Ops:
  1.3 32.6 %shard_map.103 = (bf16[256,256]{1,0:T(8,128)(2,1)S(1)}, f32[128,256]{1,0:T(8,128)S(1)}, f32[1,256]{1,0:T(1,128)S(1)}) custom-call(bf16[256,128]{1,0:T(8,128)(2,1)} %feat_hbm.1, bf16[128,256]{1,0:T(8,128)(2,1)} %weight_hbm.1, f32[1,256]{1,0:T(1,128)} %bitcast.2, bf16[256,256]{1,0:T(8,128)(2,1)} %cot_hbm.1, bf16[1,1,128,128,128]{4,3,2,1,0:T(8,128)(2,1)} %tiles_hbm.1, ...), custom_call_target="tpu_custom_call" | custom-call | tf_op jit(solution)/shard_map/pallas_call | solution.py:383
  33.9 0.0 copy-start
  33.9 0.6 %copy-done = bf16[256,256]{1,0:T(8,128)(2,1)} copy-done((bf16[256,256]{1,0:T(8,128)(2,1)}, bf16[256,256]{1,0:T(8,128)(2,1)S(1)}, u32[]{:S(2)}) %copy-start) | copy-done | bytes 131096
  34.5 0.0 copy-start.1
  34.5 0.6 %copy-done.1 = f32[128,256]{1,0:T(8,128)} copy-done((f32[128,256]{1,0:T(8,128)}, f32[128,256]{1,0:T(8,128)S(1)}, u32[]{:S(2)}) %copy-start.1) | copy-done | bytes 131096
  35.2 0.0 copy-start.2
  35.2 0.6 %copy-done.2 = f32[1,256]{1,0:T(1,128)} copy-done((f32[1,256]{1,0:T(1,128)}, f32[1,256]{1,0:T(1,128)S(1)}, u32[]{:S(2)}) %copy-start.2) | copy-done | bytes 1048
  35.7 1.7 %shard_map.104 = (bf16[256,256]{1,0:T(8,128)(2,1)}, f32[128,256]{1,0:T(8,128)}, f32[1,256]{1,0:T(1,128)}) custom-call(bf16[256,256]{1,0:T(8,128)(2,1)} %copy-done, f32[128,256]{1,0:T(8,128)} %copy-done.1, f32[1,256]{1,0:T(1,128)} %copy-done.2), custom_call_target="tpu_custom_call" | custom-call | tf_op jit(solution)/shard_map/pallas_call | solution.py:435
Async XLA Ops:
  33.9 0.7 %copy-start = (bf16[256,256]{1,0:T(8,128)(2,1)}, bf16[256,256]{1,0:T(8,128)(2,1)S(1)}, u32[]{:S(2)}) copy-start(bf16[256,256]{1,0:T(8,128)(2,1)S(1)} %get-tuple-element.9.refs_0_) | copy-start | bytes 393220
  34.5 0.6 %copy-start.1 = (f32[128,256]{1,0:T(8,128)}, f32[128,256]{1,0:T(8,128)S(1)}, u32[]{:S(2)}) copy-start(f32[128,256]{1,0:T(8,128)S(1)} %get-tuple-element.10.refs_1_) | copy-start | bytes 393220
  35.2 0.6 %copy-start.2 = (f32[1,256]{1,0:T(1,128)}, f32[1,256]{1,0:T(1,128)S(1)}, u32[]{:S(2)}) copy-start(f32[1,256]{1,0:T(1,128)S(1)} %get-tuple-element.11.refs_2_) | copy-start | bytes 3076

commit v5 on v4

--- a/solution.py
+++ b/solution.py
@@ -50,8 +50,6 @@
     index_vmem,
     index_smem,
     gathered,
-    col_part,
-    col_sibling,
     col_buf,
     col_scale,
     row_sums,
@@ -115,7 +113,13 @@
         load.start()
     barrier = pltpu.get_barrier_semaphore()
 
-    pl.semaphore_signal(barrier, inc=1, device_id=(sibling, col), device_id_type=MESH)
+    for other_level in level_flips:
+        pl.semaphore_signal(
+            barrier,
+            inc=1,
+            device_id=(other_level * 2 + 1 - core, col),
+            device_id_type=MESH,
+        )
     for other_level, other_col in others:
         pl.semaphore_signal(
             barrier,
@@ -150,7 +154,7 @@
     index_copy.start()
 
     loads[0].wait()
-    pl.semaphore_wait(barrier, chips)
+    pl.semaphore_wait(barrier, chips - 1 + levels)
 
     def feat_copy(source_row, target_row, send_slot):
         return pltpu.make_async_remote_copy(
@@ -176,7 +180,7 @@
             block = tiles[index_smem[0, a * col_tiles + b]]
             dense[a * tile : (a + 1) * tile, columns] = block
             total = total + block.astype(F32)
-        col_part[pl.ds(b, 1), :] = jnp.sum(total, axis=0, keepdims=True)
+        col_buf[row, pl.ds(b, 1), :] = jnp.sum(total, axis=0, keepdims=True)
         return carry
 
     lax.fori_loop(0, col_tiles, build, 0)
@@ -196,7 +200,53 @@
         copy.wait_send()
         copy.wait_recv()
 
-    remote(col_part, col_sibling, sibling, col, 0).start()
+    for other_level in level_flips[1:]:
+        target = other_level * 2 + core
+        remote(col_buf.at[row], col_buf.at[row], target, col, 1).start()
+    for other_level in level_flips:
+        target = other_level * 2 + 1 - core
+        remote(col_buf.at[row], col_buf.at[row], target, col, 1).start()
+
+    for step in range(1, levels):
+        source = level_flips[step] * 2 + core
+        feat_copy(source, sibling, 0).wait_recv()
+        feat_copy(source, sibling, levels + step - 1).start()
+
+    wait_all(col_buf.at[pl.ds(0, row_count - 1)], 1)
+    col_total = col_buf[0]
+    for other in range(1, row_count):
+        col_total = col_total + col_buf[other]
+    scale = jnp.concatenate(
+        [lax.rsqrt(1.0 + col_total), jnp.zeros((LANES - col_tiles, tile), F32)], axis=0
+    )
+    scale = jnp.transpose(scale)
+    for j in range(col_tiles):
+        col_scale[j] = jnp.broadcast_to(scale[:, j : j + 1], (tile, feat_width))
+
+    def scale_rows(source):
+        for i in range(feat_rows // tile):
+            j = source * (feat_rows // tile) + i
+            block = gathered[source, i * tile : (i + 1) * tile, :].astype(F32)
+            rows = pl.ds(pl.multiple_of(j * tile, tile), tile)
+            scaled[rows, :] = (col_scale[j] * block).astype(BF16)
+
+    for step in range(levels):
+        scale_rows(level_flips[step] * 2 + core)
+    feat_copy(sibling, sibling, 0).wait_recv()
+    for step in range(1, levels):
+        feat_copy(level_flips[step] * 2 + 1 - core, sibling, 0).wait_recv()
+    for step in range(levels):
+        scale_rows(level_flips[step] * 2 + 1 - core)
+
+    def piece(owner):
+        rows = pl.ds(pl.multiple_of(owner * own_rows, own_rows), own_rows)
+        return jnp.dot(dense[rows, :], scaled[...], preferred_element_type=F32)
+
+    for step in reversed(range(1, col_count)):
+        target = col_flips[step]
+        prod_send[step - 1] = piece(target).astype(WIRE)
+        remote(prod_send.at[step - 1], prod_buf.at[col], row, target, 3).start()
+    summed = piece(col)
 
     depth = 2 * feat_rows
 
@@ -208,12 +258,6 @@
         return carry
 
     row_sums[...] = jnp.zeros(row_sums.shape, F32)
-    wait_all(col_part, 0)
-    col_buf[level] = col_part[...] + col_sibling[...]
-    for step in range(1, levels):
-        target = level_flips[step] * 2 + core
-        remote(col_buf.at[level], col_buf.at[level], target, col, 1).start()
-
     lax.fori_loop(0, row_count // 2, add_rows, 0)
     for k in range(col_count):
         for at in range(0, own_rows, tile):
@@ -223,47 +267,6 @@
         target = col_flips[step]
         remote(row_send.at[target], row_buf.at[col], row, target, 2).start()
     row_buf[col] = row_send[col]
-
-    for step in range(1, levels):
-        source = level_flips[step] * 2 + core
-        feat_copy(source, sibling, 0).wait_recv()
-        feat_copy(source, sibling, levels + step - 1).start()
-
-    wait_all(col_buf.at[pl.ds(0, levels - 1)], 1)
-    col_total = col_buf[0]
-    for other in range(1, levels):
-        col_total = col_total + col_buf[other]
-    scale = jnp.concatenate(
-        [lax.rsqrt(1.0 + col_total), jnp.zeros((LANES - col_tiles, tile), F32)], axis=0
-    )
-    scale = jnp.transpose(scale)
-    for j in range(col_tiles):
-        col_scale[j] = jnp.broadcast_to(scale[:, j : j + 1], (tile, feat_width))
-
-    def scale_rows(source):
-        for i in range(feat_rows // tile):
-            j = source * (feat_rows // tile) + i
-            block = gathered[source, i * tile : (i + 1) * tile, :].astype(F32)
-            rows = pl.ds(pl.multiple_of(j * tile, tile), tile)
-            scaled[rows, :] = (col_scale[j] * block).astype(BF16)
-
-    for step in range(levels):
-        scale_rows(level_flips[step] * 2 + core)
-    feat_copy(sibling, sibling, 0).wait_recv()
-    for step in range(1, levels):
-        feat_copy(level_flips[step] * 2 + 1 - core, sibling, 0).wait_recv()
-    for step in range(levels):
-        scale_rows(level_flips[step] * 2 + 1 - core)
-
-    def piece(owner):
-        rows = pl.ds(pl.multiple_of(owner * own_rows, own_rows), own_rows)
-        return jnp.dot(dense[rows, :], scaled[...], preferred_element_type=F32)
-
-    for step in reversed(range(1, col_count)):
-        target = col_flips[step]
-        prod_send[step - 1] = piece(target).astype(WIRE)
-        remote(prod_send.at[step - 1], prod_buf.at[col], row, target, 3).start()
-    summed = piece(col)
 
     wait_all(row_buf.at[pl.ds(0, col_count - 1)], 2)
     row_total = row_buf[0]
@@ -352,15 +355,6 @@
         wgrad_ref[i * TILE_ROWS : (i + 1) * TILE_ROWS, h * LANES : (h + 1) * LANES] = out_buf[t]
 
 
-def write_out(*refs):
-    ins, outs, sems = refs[0:3], refs[3:6], refs[6]
-    stores = [pltpu.make_async_copy(ins[i], outs[i], sems.at[i]) for i in range(3)]
-    for store in stores:
-        store.start()
-    for store in stores:
-        store.wait()
-
-
 def solution(mesh):
     row_count = mesh.shape["row"]
     col_count = mesh.shape["col"]
@@ -380,7 +374,7 @@
             jax.ShapeDtypeStruct((feat_width, hidden_width), F32),
             jax.ShapeDtypeStruct((1, hidden_width), F32),
         )
-        results = pl.pallas_call(
+        hidden, weight_grad, bias_grad = pl.pallas_call(
             functools.partial(kernel, row_count, col_count),
             out_shape=shapes,
             in_specs=[hbm] * 8,
@@ -397,9 +391,7 @@
                 pltpu.VMEM((8, row_tiles * col_tiles), jnp.int32),
                 pltpu.SMEM((8, row_tiles * col_tiles), jnp.int32),
                 pltpu.VMEM((row_count, feat_rows, feat_width), BF16),
-                pltpu.VMEM((col_tiles, tile), F32),
-                pltpu.VMEM((col_tiles, tile), F32),
-                pltpu.VMEM((row_count // 2, col_tiles, tile), F32),
+                pltpu.VMEM((row_count, col_tiles, tile), F32),
                 pltpu.VMEM((col_tiles, tile, feat_width), F32),
                 pltpu.VMEM((row_tiles * tile, LANES), F32),
                 pltpu.VMEM((col_count, 8, own_rows), F32),
@@ -432,13 +424,6 @@
             tile_count,
             pltpu.with_memory_space_constraint(block_perm, pltpu.HBM),
         )
-        hidden, weight_grad, bias_grad = pl.pallas_call(
-            write_out,
-            out_shape=shapes,
-            in_specs=[vmem] * 3,
-            out_specs=(hbm, hbm, hbm),
-            scratch_shapes=[pltpu.SemaphoreType.DMA((3,))],
-        )(*results)
         return hidden, weight_grad, bias_grad.reshape(hidden_width)
 
     return jax.shard_map(

time: 37.6 us -> 38 us (1.011)
  Pallas kernels: 34.3 us -> 34.7 us
    pallas_call x1, Pallas kernels: 32.6 us -> 34.7 us  [body(): pl.pallas_call(functools.partial(kernel, row_count, col_count), out_shape...]
    pallas_call x1 -> x0, Pallas kernels: 1.69 us -> none  [body(): pl.pallas_call(write_out, out_shape=shapes, in_specs=[vmem] * 3, out_spec...]
    unnamed x6 -> x3, local copies, waits for them, and re-layouts: 1.88 us -> 1.88 us
where the time goes in v5:
time: 38 us; the launch traced here: 37.8 us
  Pallas kernels  34.7 us (91%)
  local copies, waits for them, and re-layouts  1.88 us (5%)
  between operations  1.29 us (3%)
    pallas_call x1, Pallas kernels, body(): pl.pallas_call(functools.partial(kernel, row_count, col_count), out_shape...  34.7 us
    unnamed x3, local copies, waits for them, and re-layouts  1.88 us

profile of v5, /device:TPU:0, one launch (start us, length us, event | category | flops | bytes accessed | tf_op | source)
XLA Modules:
  0.0 37.8 jit_solution(4743095846287750590)
XLA Ops:
  1.3 34.7 %shard_map.103 = (bf16[256,256]{1,0:T(8,128)(2,1)S(1)}, f32[128,256]{1,0:T(8,128)S(1)}, f32[1,256]{1,0:T(1,128)S(1)}) custom-call(bf16[256,128]{1,0:T(8,128)(2,1)} %feat_hbm.1, bf16[128,256]{1,0:T(8,128)(2,1)} %weight_hbm.1, f32[1,256]{1,0:T(1,128)} %bitcast.3, bf16[256,256]{1,0:T(8,128)(2,1)} %cot_hbm.1, bf16[1,1,128,128,128]{4,3,2,1,0:T(8,128)(2,1)} %tiles_hbm.1, ...), custom_call_target="tpu_custom_call" | custom-call | tf_op jit(solution)/shard_map/pallas_call | solution.py:377
  36.0 0.7 %copy.15 = bf16[256,256]{1,0:T(8,128)(2,1)} copy(bf16[256,256]{1,0:T(8,128)(2,1)S(1)} %get-tuple-element.12) | data formatting | bytes 262144
  36.6 0.7 %copy.16 = f32[128,256]{1,0:T(8,128)} copy(f32[128,256]{1,0:T(8,128)S(1)} %get-tuple-element.13) | data formatting | bytes 262144
  37.3 0.6 %copy.17 = f32[256]{0:T(256)} copy(f32[256]{0:T(256)S(1)} %bitcast.2) | data formatting | bytes 2048

commit v6 on v5

--- a/solution.py
+++ b/solution.py
@@ -52,7 +52,6 @@
     gathered,
     col_buf,
     col_scale,
-    row_sums,
     row_send,
     row_buf,
     scaled,
@@ -207,6 +206,23 @@
         target = other_level * 2 + 1 - core
         remote(col_buf.at[row], col_buf.at[row], target, col, 1).start()
 
+    pieces = own_rows // tile
+
+    def add_rows(a, carry):
+        rows = pl.ds(pl.multiple_of(a * tile, tile), tile)
+        total = jnp.zeros((tile, tile), F32)
+        for b in range(col_tiles):
+            total = total + dense[rows, b * tile : (b + 1) * tile].astype(F32)
+        sums = jnp.sum(jnp.transpose(total), axis=0, keepdims=True)
+        row_send[a // pieces, lax.rem(a, pieces)] = jnp.broadcast_to(sums, (8, tile))
+        return carry
+
+    lax.fori_loop(0, row_tiles, add_rows, 0)
+    for step in range(1, col_count):
+        target = col_flips[step]
+        remote(row_send.at[target], row_buf.at[col], row, target, 2).start()
+    row_buf[col] = row_send[col]
+
     for step in range(1, levels):
         source = level_flips[step] * 2 + core
         feat_copy(source, sibling, 0).wait_recv()
@@ -247,26 +263,6 @@
         prod_send[step - 1] = piece(target).astype(WIRE)
         remote(prod_send.at[step - 1], prod_buf.at[col], row, target, 3).start()
     summed = piece(col)
-
-    depth = 2 * feat_rows
-
-    def add_rows(k, carry):
-        columns = pl.ds(pl.multiple_of(k * depth, depth), depth)
-        row_sums[...] += jnp.dot(
-            dense[:, columns], jnp.ones((depth, LANES), BF16), preferred_element_type=F32
-        )
-        return carry
-
-    row_sums[...] = jnp.zeros(row_sums.shape, F32)
-    lax.fori_loop(0, row_count // 2, add_rows, 0)
-    for k in range(col_count):
-        for at in range(0, own_rows, tile):
-            sums = row_sums[k * own_rows + at : k * own_rows + at + tile, :]
-            row_send[k, :, at : at + tile] = jnp.transpose(sums)[0:8, :]
-    for step in range(1, col_count):
-        target = col_flips[step]
-        remote(row_send.at[target], row_buf.at[col], row, target, 2).start()
-    row_buf[col] = row_send[col]
 
     wait_all(row_buf.at[pl.ds(0, col_count - 1)], 2)
     row_total = row_buf[0]
@@ -276,9 +272,9 @@
     row_scale = jnp.concatenate(
         [
             jnp.transpose(
-                jnp.broadcast_to(row_scale[0:1, at : at + tile], (LANES, tile))
+                jnp.broadcast_to(row_scale[at, 0:1, :], (LANES, tile))
             )
-            for at in range(0, own_rows, tile)
+            for at in range(pieces)
         ],
         axis=0,
     )
@@ -393,9 +389,8 @@
                 pltpu.VMEM((row_count, feat_rows, feat_width), BF16),
                 pltpu.VMEM((row_count, col_tiles, tile), F32),
                 pltpu.VMEM((col_tiles, tile, feat_width), F32),
-                pltpu.VMEM((row_tiles * tile, LANES), F32),
-                pltpu.VMEM((col_count, 8, own_rows), F32),
-                pltpu.VMEM((col_count, 8, own_rows), F32),
+                pltpu.VMEM((col_count, own_rows // tile, 8, tile), F32),
+                pltpu.VMEM((col_count, own_rows // tile, 8, tile), F32),
                 pltpu.VMEM((col_tiles * tile, feat_width), BF16),
                 pltpu.VMEM((col_count - 1, own_rows, feat_width), WIRE),
                 pltpu.VMEM((col_count, own_rows, feat_width), WIRE),

time: 38 us -> 37 us (0.974)
  Pallas kernels: 34.7 us -> 33.7 us
    pallas_call x1, Pallas kernels: 34.7 us -> 33.7 us  [body(): pl.pallas_call(functools.partial(kernel, row_count, col_count), out_shape...]
where the time goes in v6:
time: 37 us; the launch traced here: 36.8 us
  Pallas kernels  33.7 us (91%)
  local copies, waits for them, and re-layouts  1.88 us (5%)
  between operations  1.29 us (3%)
    pallas_call x1, Pallas kernels, body(): pl.pallas_call(functools.partial(kernel, row_count, col_count), out_shape...  33.7 us
    unnamed x3, local copies, waits for them, and re-layouts  1.88 us

profile of v6, /device:TPU:0, one launch (start us, length us, event | category | flops | bytes accessed | tf_op | source)
XLA Modules:
  0.0 36.8 jit_solution(9628716499225344014)
XLA Ops:
  1.3 33.7 %shard_map.103 = (bf16[256,256]{1,0:T(8,128)(2,1)S(1)}, f32[128,256]{1,0:T(8,128)S(1)}, f32[1,256]{1,0:T(1,128)S(1)}) custom-call(bf16[256,128]{1,0:T(8,128)(2,1)} %feat_hbm.1, bf16[128,256]{1,0:T(8,128)(2,1)} %weight_hbm.1, f32[1,256]{1,0:T(1,128)} %bitcast.3, bf16[256,256]{1,0:T(8,128)(2,1)} %cot_hbm.1, bf16[1,1,128,128,128]{4,3,2,1,0:T(8,128)(2,1)} %tiles_hbm.1, ...), custom_call_target="tpu_custom_call" | custom-call | tf_op jit(solution)/shard_map/pallas_call | solution.py:373
  35.0 0.7 %copy.15 = bf16[256,256]{1,0:T(8,128)(2,1)} copy(bf16[256,256]{1,0:T(8,128)(2,1)S(1)} %get-tuple-element.12) | data formatting | bytes 262144
  35.6 0.7 %copy.16 = f32[128,256]{1,0:T(8,128)} copy(f32[128,256]{1,0:T(8,128)S(1)} %get-tuple-element.13) | data formatting | bytes 262144
  36.3 0.6 %copy.17 = f32[256]{0:T(256)} copy(f32[256]{0:T(256)S(1)} %bitcast.2) | data formatting | bytes 2048
